TPU v7x, 128 devices: a whole 4x4x4 slice. The times are simulated.
128 devices in a mesh: dp: 4 (over x), seq: 32 (over y, z, core).
Axes of the slice: x: 4, y: 4, z: 4, core: 2. Of those that a mesh axis runs over, the one named last changes fastest.
Arguments:
- activations: bfloat16 [4, 4352, 1024], P('dp', 'seq'), may hold values from -6 to 6
- qkv_weight: bfloat16 [1024, 1536], replicated, may hold values from -1 to 1
- out_weight: bfloat16 [512, 1024], replicated, may hold values from -0.25 to 0.25
- out_grad: bfloat16 [4, 4352, 1024], P('dp', 'seq'), may hold values from -6 to 6
Outputs:
- attended: bfloat16 [4, 4352, 1024], P('dp', 'seq')
- input_grad: bfloat16 [4, 4352, 1024], P('dp', 'seq')
- qkv_weight_grad: float32 [1024, 1536], P(('dp', 'seq'))
- out_weight_grad: float32 [512, 1024], P(None, ('dp', 'seq'))
All inputs are finite; a program needn't handle non-finite values.
Results may differ from a plain program's by a relative error of at most 0.04.
Values may be sent and summed in bfloat16 or wider, within the bound.
A program may use at most 192 MiB of HBM per device.

v0:
```python
from functools import partial
import math

import jax
import jax.numpy as jnp
import numpy as np
from jax import lax
from jax.sharding import PartitionSpec as P

HEADS = 8
LEVELS = 14


scale_sides = (1, 2, 3, 4, 5, 8, 9, 10, 14, 16, 20, 24, 32, 40)
masked_score = -1e30
block_keys = 1024


def token_levels(positions):
    bounds = jnp.asarray(
        np.cumsum([side_len * side_len for side_len in scale_sides[:LEVELS]])[:-1], dtype=jnp.int32
    )
    return jnp.sum((positions[:, None] >= bounds[None, :]).astype(jnp.int32), axis=1)


def score_grads(
    query_heads, grad_heads, log_totals, dots_heads, key_part, value_part, allowed, score_scale
):
    scores = (
        jnp.einsum("bgqhd,bkhd->bghqk", query_heads, key_part, preferred_element_type=jnp.float32)
        * score_scale
    )
    scores = jnp.where(allowed[None, :, None], scores, masked_score)
    probs_full = jnp.exp(scores - log_totals[..., None])
    prob_grad = jnp.einsum(
        "bgqhd,bkhd->bghqk", grad_heads, value_part, preferred_element_type=jnp.float32
    )
    score_grad = (probs_full * (prob_grad - dots_heads[..., None]) * score_scale).astype(
        jnp.bfloat16
    )
    return (probs_full.astype(jnp.bfloat16), score_grad)


def shards(activations, qkv_weight, out_weight, out_grad):
    images, row_count, model_width = activations.shape
    inner_width = out_weight.shape[0]
    head_dim = inner_width // HEADS
    score_scale = 1.0 / math.sqrt(head_dim)
    own_first = lax.axis_index("seq") * row_count
    own_levels = token_levels(own_first + jnp.arange(row_count, dtype=jnp.int32))
    projected = jnp.einsum(
        "btd,de->bte", activations, qkv_weight, preferred_element_type=jnp.float32
    ).astype(jnp.bfloat16)
    queries = projected[:, :, :inner_width]
    own_kv = projected[:, :, inner_width:]
    every_kv = lax.all_gather(own_kv, "seq", axis=1, tiled=True)
    key_total = every_kv.shape[1]
    key_levels = token_levels(jnp.arange(key_total, dtype=jnp.int32))
    block_size = math.gcd(key_total, block_keys)
    block_starts = list(range(0, key_total, block_size))
    highest = jnp.max(own_levels)
    query_heads = queries.reshape(images, 1, row_count, HEADS, head_dim)

    def block_operands(first_key):
        key_part = every_kv[:, first_key : first_key + block_size, :inner_width].reshape(
            images, block_size, HEADS, head_dim
        )
        value_part = every_kv[:, first_key : first_key + block_size, inner_width:].reshape(
            images, block_size, HEADS, head_dim
        )
        allowed = (key_levels[first_key : first_key + block_size][None, :] <= own_levels[:, None])[
            None
        ]
        return (key_part, value_part, allowed)

    def forward_block(softmax_state, first_key):
        row_max, row_sum, weighted = softmax_state
        key_part, value_part, allowed = block_operands(first_key)
        scores = (
            jnp.einsum(
                "bgqhd,bkhd->bghqk", query_heads, key_part, preferred_element_type=jnp.float32
            )
            * score_scale
        )
        scores = jnp.where(allowed[None, :, None], scores, masked_score)
        new_max = jnp.maximum(row_max, jnp.max(scores, axis=4))
        rescale = jnp.exp(row_max - new_max)
        weights = jnp.exp(scores - new_max[..., None])
        new_sum = row_sum * rescale + jnp.sum(weights, axis=4)
        new_weighted = weighted * rescale[..., None] + jnp.einsum(
            "bghqk,bkhd->bghqd",
            weights.astype(jnp.bfloat16),
            value_part,
            preferred_element_type=jnp.float32,
        )
        return (new_max, new_sum, new_weighted)

    softmax_state = (
        jnp.full((images, 1, HEADS, row_count), masked_score, jnp.float32),
        jnp.zeros((images, 1, HEADS, row_count), jnp.float32),
        jnp.zeros((images, 1, HEADS, row_count, head_dim), jnp.float32),
    )
    for first_key in block_starts:
        is_live = key_levels[first_key] <= highest
        softmax_state = lax.cond(
            is_live,
            partial(forward_block, first_key=first_key),
            lambda kept_state: kept_state,
            softmax_state,
        )
    row_max, row_sum, weighted = softmax_state
    log_totals = row_max + jnp.log(row_sum)
    context = (
        (weighted / row_sum[..., None])
        .astype(jnp.bfloat16)[:, 0]
        .transpose(0, 2, 1, 3)
        .reshape(images, row_count, inner_width)
    )
    attended = jnp.einsum(
        "bth,hd->btd", context, out_weight, preferred_element_type=jnp.float32
    ).astype(jnp.bfloat16)
    context_grad = jnp.einsum(
        "btd,hd->bth", out_grad, out_weight, preferred_element_type=jnp.float32
    ).astype(jnp.bfloat16)
    row_dots = jnp.sum(
        (context_grad.astype(jnp.float32) * context.astype(jnp.float32)).reshape(
            images, row_count, HEADS, head_dim
        ),
        axis=3,
    )
    grad_heads = context_grad.reshape(images, 1, row_count, HEADS, head_dim)
    dots_heads = row_dots.transpose(0, 2, 1)[:, None]
    term_shape = (images, block_size, 2 * inner_width)

    def backward_block(grad_sum, first_key):
        key_part, value_part, allowed = block_operands(first_key)
        probs_low, score_grad = score_grads(
            query_heads,
            grad_heads,
            log_totals,
            dots_heads,
            key_part,
            value_part,
            allowed,
            score_scale,
        )
        grad_sum = grad_sum + jnp.einsum(
            "bghqk,bkhd->bgqhd", score_grad, key_part, preferred_element_type=jnp.float32
        )
        key_grad = jnp.einsum(
            "bghqk,bgqhd->bkhd", score_grad, query_heads, preferred_element_type=jnp.float32
        ).reshape(images, block_size, inner_width)
        value_grad = jnp.einsum(
            "bghqk,bgqhd->bkhd", probs_low, grad_heads, preferred_element_type=jnp.float32
        ).reshape(images, block_size, inner_width)
        block_term = jnp.concatenate([key_grad, value_grad], axis=2)
        return (grad_sum, block_term)

    def skipped_block(grad_sum, first_key):
        return (grad_sum, jnp.zeros(term_shape, jnp.float32))

    query_grad = jnp.zeros((images, 1, row_count, HEADS, head_dim), jnp.float32)
    key_terms = []
    for first_key in block_starts:
        is_live = key_levels[first_key] <= highest
        query_grad, block_term = lax.cond(
            is_live,
            partial(backward_block, first_key=first_key),
            partial(skipped_block, first_key=first_key),
            query_grad,
        )
        key_terms.append(block_term)
    key_term = jnp.concatenate(key_terms, axis=1)
    kv_grad = lax.psum_scatter(
        key_term.astype(jnp.bfloat16), "seq", scatter_dimension=1, tiled=True
    )
    query_low = query_grad[:, 0].reshape(images, row_count, inner_width).astype(jnp.bfloat16)
    qkv_grad = jnp.concatenate([query_low, kv_grad], axis=2)
    input_grad = jnp.einsum(
        "bte,de->btd", qkv_grad, qkv_weight, preferred_element_type=jnp.float32
    ).astype(jnp.bfloat16)
    input_part = jnp.einsum(
        "btd,bte->de", activations, qkv_grad, preferred_element_type=jnp.float32
    )
    output_part = jnp.einsum("btd,bth->dh", out_grad, context, preferred_element_type=jnp.float32)
    weight_sums = lax.psum_scatter(
        jnp.concatenate([input_part, output_part], axis=1),
        ("dp", "seq"),
        scatter_dimension=0,
        tiled=True,
    )
    qkv_weight_grad = weight_sums[:, : 3 * inner_width]
    out_weight_grad = weight_sums[:, 3 * inner_width :].T
    return (attended, input_grad, qkv_weight_grad, out_weight_grad)


def solution(mesh):
    return jax.shard_map(
        shards,
        mesh=mesh,
        in_specs=(P("dp", "seq", None), P(), P(), P("dp", "seq", None)),
        out_specs=(
            P("dp", "seq", None),
            P("dp", "seq", None),
            P(("dp", "seq"), None),
            P(None, ("dp", "seq")),
        ),
        check_vma=False,
    )
```

profile of v0, /device:TPU:1, one launch (start us, length us, event | category | flops | bytes accessed | tf_op | source)
XLA Modules:
  0.0 1681.0 jit_solution(11769001456950053467)
XLA Ops:
  37.3 33.0 %all-gather.2.cloned.1.call-done = bf16[1,4352,1024]{2,1,0:T(8,128)(2,1)} async-done(((bf16[1,136,1024]{2,1,0:T(8,128)(2,1)}), bf16[1,4352,1024]{2,1,0:T(8,128)(2,1)}) %all-gather.2.cloned.1.call-update) | async-done | bytes 8912912 | tf_op jit(solution)/shard_map/all_gather | solution.py:56
  70.3 18.0 %conditional.34 = (f32[1,1,8,136]{3,2,1,0:T(8,128)S(1)}, f32[1,1,8,136]{3,2,1,0:T(8,128)S(1)}, f32[1,1,8,136,64]{3,4,2,1,0:T(8,128)}) conditional(s32[]{:T(128)} %convert_element_type.301, () %tuple.248, (s32[4352]{0:T(1024)S(1)}, s32[136]{0:T(256)S(1)}, bf16[1,4352,1024]{2,1,0:T(8,128)(2,1)}, bf16[1,1,136,8,64]{4,3,2,1,0:T(8,128)(2,1)S(1)}) %tuple.249), branch_computations={%region_3.0_spmd, %region_4.7_spmd} | conditional | flops 73362752 | bytes 24611412 | solution.py:105
  70.3 11.7 copy.291
  88.3 19.2 %conditional.35 = ((f32[1,1,8,136]{3,2,1,0:T(8,128)S(1)}, f32[1,1,8,136]{3,2,1,0:T(8,128)S(1)}, f32[1,1,8,136,64]{3,4,2,1,0:T(8,128)})) conditional(s32[]{:T(128)} %convert_element_type.300, (f32[1,1,8,136]{3,2,1,0:T(8,128)S(1)}, f32[1,1,8,136]{3,2,1,0:T(8,128)S(1)}, f32[1,1,8,136,64]{3,4,2,1,0:T(8,128)}) %conditional.34, (s32[4352]{0:T(1024)S(1)}, ...), branch_computations={%region_7.8_spmd, %region_8.11_spmd} | conditional | flops 73430208 | bytes 24907356 | solution.py:105
  88.3 11.8 copy.293
  107.8 8.4 conditional.45
  116.9 6.5 conditional.50
  126.9 2.5 convert_multiply_fusion
  134.5 23.5 %conditional.51 = (f32[1,1,136,8,64]{2,4,3,1,0:T(8,128)}, bf16[1,256,1024]{1,2,0:T(8,128)(2,1)S(1)}) conditional(s32[]{:T(128)} %convert_element_type.301, () %tuple.266, (s32[4352]{0:T(1024)S(1)}, s32[136]{0:T(256)S(1)}, bf16[1,4352,1024]{2,1,0:T(8,128)(2,1)}, bf16[1,1,136,8,64]{4,3,2,1,0:T(8,128)(2,1)S(1)}, f32[1,1,8,136]{3,2,1,0:T(8,128)S(1)}, ...), branch_computations={%region_72.73_spmd, %region_73.74_spmd} | conditional | flops 181569536 | bytes 36446908 | solution.py:166
  134.5 11.8 copy.326
  149.2 2.5 fusion.169
  158.8 24.6 %conditional.52 = (f32[1,1,136,8,64]{2,4,3,1,0:T(8,128)}, bf16[1,256,1024]{1,2,0:T(8,128)(2,1)}) conditional(s32[]{:T(128)} %convert_element_type.300, f32[1,1,136,8,64]{2,4,3,1,0:T(8,128)} %get-tuple-element.1005, (s32[4352]{0:T(1024)S(1)}, s32[136]{0:T(256)S(1)}, bf16[1,4352,1024]{2,1,0:T(8,128)(2,1)}, ...), branch_computations={%region_74.75_spmd, %region_75.76_spmd} | conditional | flops 181639168 | bytes 34628256 | solution.py:166
  158.8 11.7 copy.330
  173.4 2.5 fusion.187
  189.4 4.7 conditional.60
  197.6 3.6 conditional.65
  236.3 37.0 %copy.397 = bf16[1,4352,1024]{2,0,1:T(2,128)(2,1)} copy(bf16[1,4352,1024]{1,2,0:T(8,128)(2,1)} %constant_dynamic-update-slice_fusion) | data formatting | bytes 17825792
  273.3 12.6 copy.408
  288.0 2.7 convolution_bitcast_fusion.52
  290.7 714.8 %reduce-scatter.7.cloned.1.call-done = bf16[136,1024]{1,0:T(8,128)(2,1)} async-done(((bf16[4352,1024]{1,0:T(8,128)(2,1)}), bf16[136,1024]{1,0:T(8,128)(2,1)}) %reduce-scatter.7.cloned.1.call-update) | async-done | bytes 278544
  1011.7 6.3 pad_maximum_fusion
  1017.9 9.2 copy.399
  1027.2 2.3 fusion.495
  1031.4 640.1 %reduce-scatter.9.cloned.1.call-done = f32[8,2048]{1,0:T(8,128)} async-done(((f32[1024,2048]{1,0:T(8,128)}), f32[8,2048]{1,0:T(8,128)}) %reduce-scatter.9.cloned.1.call-update) | async-done | bytes 65552
  (164 shorter events, 123.8 us)
Async XLA Ops:
  7.2 1.9 copy-start
  7.2 63.1 %all-gather.2.cloned.1.call-start = ((), (), s32[]{:S(2)}) async-start(), calls=%async_computation.2 | async-start | bytes 9191424 | tf_op jit(solution)/shard_map/all_gather | solution.py:56
  10.6 0.8 copy-start.40
  11.4 3.5 copy-start.93
  12.1 993.3 %reduce-scatter.7.cloned.1.call-start = ((), (), s32[]{:S(2)}) async-start(), calls=%async_computation.3 | async-start | bytes 9191424
  84.8 1.7 copy-start.92
  103.0 2.3 copy-start.42
  153.6 1.9 copy-start.74
  153.6 2.2 copy-start.2
  153.6 2.2 copy-start.20
  155.8 1.1 copy-start.91
  156.9 1.1 copy-start.38
  158.0 0.8 copy-start.39
  177.9 1.9 copy-start.75
  177.9 2.2 copy-start.3
  177.9 2.2 copy-start.21
  180.0 1.1 copy-start.57
  285.9 2.1 copy-start.19
  285.9 1385.6 %reduce-scatter.9.cloned.1.call-start = ((), (), s32[]{:S(2)}) async-start(), calls=%async_computation.4 | async-start | bytes 8454144
  1027.1 2.4 copy-start.37
  1027.1 2.4 copy-start.41
Sparse Core Ops, SparseCore 0:
  12.3 57.9 all-gather.1
  286.1 719.3 reduce-scatter.6
  1027.3 644.1 reduce-scatter.8
where the time goes:
time: 1710 us; the launch traced here: 1680 us
  waiting for transfers between devices  1390 us (81%)
  local copies, waits for them, and re-layouts  187 us (11%)
  between operations  35.1 us (2%)
  matrix products  32.8 us (2%)
  loops' own time  21.7 us (1%)
    unnamed x5, waiting for transfers between devices  1350 us
    unnamed x35, local copies, waits for them, and re-layouts  97.6 us
    another operation x28, local copies, waits for them, and re-layouts  69 us
  transfers between devices with their start and end apart: 3, of which 3 were waited for; matrix products, arithmetic and copies ran while one was open for 1% of the time, Pallas kernels for 0%

commit v1 on v0

v1 whole, which is shorter than its diff:
```python
import functools
import math

import jax
import jax.numpy as jnp
import numpy as np
from jax import lax
from jax.experimental import pallas as pl
from jax.experimental.pallas import tpu as pltpu
from jax.sharding import PartitionSpec as P

MESH = pl.DeviceIdType.MESH
BF = jnp.bfloat16
F32 = jnp.float32

HEADS = 8
SEQ = 32
TOK = 136
PAD = 144
KEYS = SEQ * PAD
D = 1024
INNER = 512
SIDES = (1, 2, 3, 4, 5, 8, 9, 10, 14, 16, 20, 24, 32, 40)
ENDS = [int(v) for v in np.cumsum([a * a for a in SIDES])]
STARTS = [0] + ENDS[:-1]
FAR = 1 << 20
BIG = 1e30
ONE = 15
TWO = 16
CHUNK = 512
BATCHES = (
    (0, 3 * PAD, 4608),
    (3 * PAD, 2 * PAD, 3072),
    (5 * PAD, PAD, 2048),
    (6 * PAD, PAD, 1536),
    (7 * PAD, PAD, 1024),
)
ORDERS = ("xyz", "yzx", "zxy")
COLS = ((0, 384), (384, 384), (768, 256))
NT = (((1,), (1,)), ((), ()))


def dot(a, b):
    return jnp.dot(a, b, preferred_element_type=F32)


def dot_nt(a, b):
    return lax.dot_general(a, b, NT, preferred_element_type=F32)


def lane_bounds(rows):
    lane = lax.broadcasted_iota(jnp.int32, (rows, 128), 1)
    lo = jnp.full((rows, 128), -1, jnp.int32)
    hi = jnp.full((rows, 128), -1, jnp.int32)
    for i, (a, b) in enumerate(zip(STARTS, ENDS)):
        lo = jnp.where(lane == i, a, lo)
        hi = jnp.where(lane == i, b, hi)
    lo = jnp.where(lane == 14, FAR, lo)
    hi = jnp.where(lane == 14, FAR + 1, hi)
    ones = (lane == ONE) | (lane == TWO)
    lo = jnp.where(ones, 0, lo)
    hi = jnp.where(ones, ENDS[-1], hi)
    return lo, hi


def swap_pack(a, b, left):
    return (
        jnp.where(left, a, pltpu.roll(b, 64, 1)),
        jnp.where(left, pltpu.roll(a, 64, 1), b),
    )


def kernel(act_h, wqkv_h, wout_h, og_h, att_o, ing_o, wq_o, wo_o,
           al, alT, wqkv, wout, sendkv, sendqg, kvx, qg, qx, sbuf, pbuf, macc, acc, dq,
           qgT, dkT, dkvb, sibr, resb, rqc, rkv, catb, fb,
           r1a, r1b, r1c, g1a, g1b, g1c, r2a, r2b, r2c, g2a, g2b, g2c, r3a, r3b, r3c,
           fin, lsem, ssem, rsem, fs, fr):
    x = lax.axis_index("dp")
    s = lax.axis_index("seq")
    head, quarter = s // 4, s % 4
    pos, core = s // 2, s % 2
    y, z = s // 8, (s // 2) % 4
    sib = s + 1 - 2 * core

    cin = [
        pltpu.make_async_copy(act_h.at[0], al.at[0, pl.ds(0, TOK)], lsem.at[0]),
        pltpu.make_async_copy(wqkv_h, wqkv, lsem.at[1]),
        pltpu.make_async_copy(og_h.at[0], al.at[1, pl.ds(0, TOK)], lsem.at[2]),
        pltpu.make_async_copy(wout_h, wout, lsem.at[3]),
    ]
    for c in cin:
        c.start()

    bar = pltpu.get_barrier_semaphore()

    @pl.loop(1, 16)
    def _(k):
        pl.semaphore_signal(bar, inc=1, device_id=(x, 2 * ((pos + k) % 16) + core), device_id_type=MESH)

    pl.semaphore_signal(bar, inc=1, device_id=(x, sib), device_id_type=MESH)
    for k in range(1, 4):
        pl.semaphore_signal(bar, inc=1, device_id=((x + k) % 4, s), device_id_type=MESH)

    al[0, TOK:PAD, :] = jnp.zeros((PAD - TOK, D), BF)
    al[1, TOK:PAD, :] = jnp.zeros((PAD - TOK, D), BF)
    pl.semaphore_wait(bar, 19)

    def remote(src, dst, send, recv, dev):
        return pltpu.make_async_remote_copy(
            src_ref=src, dst_ref=dst, send_sem=send, recv_sem=recv, device_id=dev, device_id_type=MESH)

    def rows(ref, first, count=PAD):
        return ref.at[pl.ds(pl.multiple_of(first, 16), count)]

    def kvslot(g):
        return kvx.at[pl.ds(pl.multiple_of(g * PAD, 16), PAD), pl.ds(0, 128)]

    left = lax.broadcasted_iota(jnp.int32, (PAD, 128), 1) < 64

    cin[0].wait()
    cin[1].wait()
    kp = dot(al[0, 0:PAD, :], wqkv[:, INNER:2 * INNER])
    vp = dot(al[0, 0:PAD, :], wqkv[:, 2 * INNER:])
    for i in range(4):
        a, b = swap_pack(kp[:, 128 * i:128 * i + 128], vp[:, 128 * i:128 * i + 128], left)
        sendkv[(2 * i) * PAD:(2 * i + 1) * PAD, :] = a.astype(BF)
        sendkv[(2 * i + 1) * PAD:(2 * i + 2) * PAD, :] = b.astype(BF)

    own_kv = pltpu.make_async_copy(rows(sendkv, head * PAD), kvslot(s), lsem.at[4])
    own_kv.start()

    @pl.loop(1, 16)
    def _(k):
        to = (pos + k) % 16
        remote(rows(sendkv, (to // 2) * PAD), kvslot(s), ssem.at[0], rsem.at[0], (x, 2 * to + core)).start()

    cin[2].wait()
    cin[3].wait()
    qp = dot(al[0, 0:PAD, :], wqkv[:, 0:INNER])
    gp = dot_nt(al[1, 0:PAD, :], wout[...])
    for i in range(4):
        a, b = swap_pack(qp[:, 128 * i:128 * i + 128], gp[:, 128 * i:128 * i + 128], left)
        sendqg[(2 * i) * PAD:(2 * i + 1) * PAD, :] = a.astype(BF)
        sendqg[(2 * i + 1) * PAD:(2 * i + 2) * PAD, :] = b.astype(BF)

    slot = 7 - s // 4
    own_qg = pltpu.make_async_copy(rows(sendqg, head * PAD), rows(qg, slot * PAD), lsem.at[5])
    own_qg.start()

    @pl.loop(1, 8)
    def _(k):
        to = (head + k) % 8
        remote(rows(sendqg, to * PAD), rows(qg, slot * PAD), ssem.at[1], rsem.at[1], (x, 4 * to + quarter)).start()

    inputs_to_sib = remote(al.at[:, pl.ds(0, PAD)], al.at[:, pl.ds(PAD, PAD)], ssem.at[2], rsem.at[2], (x, sib))
    inputs_to_sib.start()

    lo, hi = lane_bounds(PAD)
    place = lax.broadcasted_iota(jnp.int32, (PAD, 128), 0)

    @pl.loop(0, SEQ)
    def _(g):
        t = jnp.where(place < TOK, place + g * TOK, FAR)
        kvx[pl.ds(pl.multiple_of(g * PAD, 16), PAD), 128:256] = jnp.where(
            (t >= lo) & (t < hi), 1.0, 0.0).astype(BF)

    own_kv.wait()
    remote(rows(dkvb, 0, 15 * PAD), rows(dkvb, 0, 15 * PAD), ssem.at[0], rsem.at[0], (x, sib)).wait_recv()

    @pl.loop(0, 16)
    def _(k):
        g = 2 * k + core
        remote(kvslot(g), kvslot(g), ssem.at[3], rsem.at[3], (x, sib)).start()

    own_qg.wait()
    remote(rows(dkvb, 0, 7 * PAD), rows(dkvb, 0, 7 * PAD), ssem.at[1], rsem.at[1], (x, sib)).wait_recv()

    @pl.loop(0, 8)
    def _(j):
        g = 4 * (7 - j) + quarter
        t = jnp.where(place < TOK, place + g * TOK, ENDS[-1] - 1)
        r = pl.ds(pl.multiple_of(j * PAD, 16), PAD)
        qx[r, 128:256] = jnp.where(lo > t, -BIG, 0.0).astype(BF)
        qx[r, 0:128] = jnp.where(left, qg[r, :].astype(F32) * 0.125, 0.0).astype(BF)

    remote(rows(dkvb, 0, 16 * PAD), rows(dkvb, 0, 16 * PAD), ssem.at[3], rsem.at[3], (x, sib)).wait()

    for number, (row0, count, keys) in enumerate(BATCHES):
        rr = slice(row0, row0 + count)
        steps = keys // CHUNK
        macc[0:count, :] = jnp.full((count, 128), -3e38, F32)

        @pl.loop(0, steps)
        def _(c):
            kk = pl.ds(pl.multiple_of(c * CHUNK, CHUNK), CHUNK)
            sc = dot_nt(qx[rr, :], kvx[kk, :])
            sbuf[0:count, kk] = sc
            top = macc[0:count, :]
            for i in range(CHUNK // 128):
                top = jnp.maximum(top, sc[:, 128 * i:128 * i + 128])
            macc[0:count, :] = top

        row_max = jnp.max(macc[0:count, :], axis=1, keepdims=True)
        acc[0:count, :] = jnp.zeros((count, 256), F32)

        @pl.loop(0, steps)
        def _(c):
            kk = pl.ds(pl.multiple_of(c * CHUNK, CHUNK), CHUNK)
            p = jnp.exp(sbuf[0:count, kk] - row_max).astype(BF)
            pbuf[0:count, kk] = p
            acc[0:count, :] += dot(p, kvx[kk, :])

        lane = lax.broadcasted_iota(jnp.int32, (count, 128), 1)
        near = lane < 64
        inv = 1.0 / acc[0:count, 128 + ONE:128 + ONE + 1]
        ctx = (acc[0:count, 0:128] * inv).astype(BF)
        qrow = qg[rr, :].astype(F32)
        dots = jnp.sum(jnp.where(near, 0.0, ctx.astype(F32) * qrow), axis=1, keepdims=True)
        dhi = dots.astype(BF).astype(F32)
        dlo = dots - dhi
        qx[rr, 0:128] = jnp.where(near, 0.0, qrow).astype(BF)
        qx[rr, 128:256] = jnp.where(lane == ONE, -dhi, jnp.where(lane == TWO, -dlo, 0.0)).astype(BF)
        qn = qrow * jnp.where(near, 0.125 * inv, inv)
        qgT[:, 0:count] = qn.T.astype(BF)
        dq[0:count, :] = jnp.zeros((count, 128), F32)

        @pl.loop(0, steps)
        def _(c):
            kk = pl.ds(pl.multiple_of(c * CHUNK, CHUNK), CHUNK)
            p = pbuf[0:count, kk]
            dpd = dot_nt(qx[rr, :], kvx[kk, :])
            ds = (p.astype(F32) * dpd).astype(BF)
            dq[0:count, :] += dot(ds, kvx[kk, 0:128])
            dk = dot(qgT[0:64, 0:count], ds)
            dv = dot(qgT[64:128, 0:count], p)
            if number == 0:
                dkT[0:64, kk] = dk
                dkT[64:128, kk] = dv
            else:
                dkT[0:64, kk] += dk
                dkT[64:128, kk] += dv

        resb[rr, :] = jnp.where(near, dq[0:count, :] * (0.125 * inv), ctx.astype(F32)).astype(BF)

    own_res = pltpu.make_async_copy(rows(resb, slot * PAD), rows(rqc, head * PAD), lsem.at[6])
    own_res.start()

    @pl.loop(1, 8)
    def _(k):
        to = (head + k) % 8
        remote(rows(resb, (7 - to) * PAD), rows(rqc, head * PAD), ssem.at[4], rsem.at[4],
               (x, 4 * to + quarter)).start()

    @pl.loop(0, KEYS // CHUNK)
    def _(c):
        kk = pl.ds(pl.multiple_of(c * CHUNK, CHUNK), CHUNK)
        dkvb[kk, :] = dkT[:, kk].T.astype(BF)

    @pl.loop(0, 16)
    def _(k):
        g = 2 * k + 1 - core
        remote(rows(dkvb, g * PAD), rows(sibr, g * PAD), ssem.at[5], rsem.at[5], (x, sib)).start()

    remote(rows(dkvb, 0, 16 * PAD), rows(sibr, 0, 16 * PAD), ssem.at[5], rsem.at[5], (x, sib)).wait_recv()

    @pl.loop(0, 16)
    def _(k):
        r = pl.ds(pl.multiple_of((2 * k + core) * PAD, 16), PAD)
        dkvb[r, :] = (dkvb[r, :].astype(F32) + sibr[r, :].astype(F32)).astype(BF)

    part = 2 * head + (pos % 2)
    own_dkv = pltpu.make_async_copy(rows(dkvb, s * PAD), rows(rkv, part * PAD), lsem.at[7])
    own_dkv.start()

    @pl.loop(1, 16)
    def _(k):
        to = 2 * ((pos + k) % 16) + core
        remote(rows(dkvb, to * PAD), rows(rkv, part * PAD), ssem.at[6], rsem.at[6], (x, to)).start()

    inputs_to_sib.wait()
    for i in range(2):
        for j in range(8):
            alT[i, 128 * j:128 * j + 128, :] = al[i, :, 128 * j:128 * j + 128].T

    own_res.wait()
    remote(rows(rqc, 0, 7 * PAD), rows(rqc, 0, 7 * PAD), ssem.at[4], rsem.at[4], (x, sib)).wait()
    for i in range(4):
        a = rqc[(2 * i) * PAD:(2 * i + 1) * PAD, :].astype(F32)
        b = rqc[(2 * i + 1) * PAD:(2 * i + 2) * PAD, :].astype(F32)
        q_pair, c_pair = swap_pack(a, b, left)
        catb[0, 0:PAD, 128 * i:128 * i + 128] = q_pair.astype(BF)
        catb[3, 0:PAD, 128 * i:128 * i + 128] = c_pair.astype(BF)
    att = dot(catb[3, 0:PAD, :], wout[...])
    att_o[0] = att[0:TOK].astype(BF)

    own_dkv.wait()
    remote(rows(rkv, 0, 15 * PAD), rows(rkv, 0, 15 * PAD), ssem.at[6], rsem.at[6], (x, sib)).wait()
    for i in range(4):
        a = rkv[(4 * i) * PAD:(4 * i + 1) * PAD, :].astype(F32) + rkv[(4 * i + 1) * PAD:(4 * i + 2) * PAD, :].astype(F32)
        b = rkv[(4 * i + 2) * PAD:(4 * i + 3) * PAD, :].astype(F32) + rkv[(4 * i + 3) * PAD:(4 * i + 4) * PAD, :].astype(F32)
        k_pair, v_pair = swap_pack(a, b, left)
        catb[1, 0:PAD, 128 * i:128 * i + 128] = k_pair.astype(BF)
        catb[2, 0:PAD, 128 * i:128 * i + 128] = v_pair.astype(BF)

    cat_to_sib = remote(catb.at[pl.ds(2 - 2 * core, 2), pl.ds(0, PAD)], catb.at[pl.ds(2 - 2 * core, 2), pl.ds(PAD, PAD)],
                        ssem.at[7], rsem.at[7], (x, sib))
    cat_to_sib.start()
    ing = dot_nt(catb[0, 0:PAD, :], wqkv[:, 0:INNER])
    ing += dot_nt(catb[1, 0:PAD, :], wqkv[:, INNER:2 * INNER])
    ing += dot_nt(catb[2, 0:PAD, :], wqkv[:, 2 * INNER:])
    ing_o[0] = ing[0:TOK].astype(BF)
    cat_to_sib.wait()

    for half in range(2):
        which = 0 if half == 0 else core
        right = catb[2 * core + half]

        @pl.loop(0, 4)
        def _(i):
            f = dot(alT[which, pl.ds(pl.multiple_of(i * 256, 256), 256), :], right)
            fb[i, :, :, :, INNER * half:INNER * half + INNER] = f.astype(BF).reshape(4, 4, 16, INNER)

    coords = {"x": x, "y": y, "z": z}

    def peer(axis, k):
        c = dict(coords)
        c[axis] = (coords[axis] + k) % 4
        return c[axis], (c["x"], c["y"] * 8 + c["z"] * 2 + core)

    def stage(o, phase, take, recv):
        for k in range(1, 4):
            there, dev = peer(ORDERS[o][phase], k)
            remote(take(there), recv.at[k - 1], fs.at[3 * phase + o], fr.at[3 * phase + o], dev).start()

    def arrived(o, phase, recv):
        remote(recv, recv, fs.at[3 * phase + o], fr.at[3 * phase + o], (x, sib)).wait()

    def total(mine, recv):
        v = mine.astype(F32)
        for k in range(3):
            v += recv[k].astype(F32)
        return v

    def cols(o):
        return pl.ds(*COLS[o])

    takes1 = (
        lambda t: fb.at[t, :, :, :, cols(0)],
        lambda t: fb.at[:, t, :, :, cols(1)],
        lambda t: fb.at[:, :, t, :, cols(2)],
    )
    r1, g1 = (r1a, r1b, r1c), (g1a, g1b, g1c)
    r2, g2 = (r2a, r2b, r2c), (g2a, g2b, g2c)
    r3 = (r3a, r3b, r3c)
    takes2 = (lambda t: g1a.at[t], lambda t: g1b.at[:, t], lambda t: g1c.at[t])
    for o in range(3):
        stage(o, 0, takes1[o], r1[o])
    for o in range(3):
        arrived(o, 0, r1[o])
        mine = coords[ORDERS[o][0]]
        g1[o][...] = total(takes1[o](mine)[...], r1[o]).astype(BF)
        stage(o, 1, takes2[o], r2[o])
    for o in range(3):
        arrived(o, 1, r2[o])
        mine = coords[ORDERS[o][1]]
        g2[o][...] = total(takes2[o](mine)[...], r2[o]).astype(BF)
        stage(o, 2, lambda t, o=o: g2[o].at[t], r3[o])
    for o in range(3):
        arrived(o, 2, r3[o])
        mine = coords[ORDERS[o][2]]
        v = total(g2[o][mine], r3[o])
        a, n = COLS[o]
        fin[core, 0, :, a:a + n] = v[0:8]
        fin[core, 1, :, a:a + n] = v[8:16]

    last = remote(fin.at[core, 1 - core], fin.at[core, 1 - core], ssem.at[8], rsem.at[8], (x, sib))
    last.start()
    last.wait()
    wq_o[:, 0:D] = fin[0, core]
    wq_o[:, D:] = fin[1, core, :, 0:INNER]
    wo_o[...] = fin[1, core, :, INNER:]

    remote(rows(dkvb, 0, 15 * PAD), rows(dkvb, 0, 15 * PAD), ssem.at[0], rsem.at[0], (x, sib)).wait_send()
    remote(rows(dkvb, 0, 7 * PAD), rows(dkvb, 0, 7 * PAD), ssem.at[1], rsem.at[1], (x, sib)).wait_send()
    remote(rows(dkvb, 0, 16 * PAD), rows(dkvb, 0, 16 * PAD), ssem.at[5], rsem.at[5], (x, sib)).wait_send()


def shards(activations, qkv_weight, out_weight, out_grad):
    any_spec = pl.BlockSpec(memory_space=pl.ANY)
    vmem = pl.BlockSpec(memory_space=pltpu.VMEM)
    V = pltpu.VMEM
    widths = [c[1] for c in COLS]
    scratch = [
        V((2, 2 * PAD, D), BF),
        V((2, D, 2 * PAD), BF),
        V((D, 3 * INNER), BF),
        V((INNER, D), BF),
        V((8 * PAD, 128), BF),
        V((8 * PAD, 128), BF),
        V((KEYS, 256), BF),
        V((8 * PAD, 128), BF),
        V((8 * PAD, 256), BF),
        V((3 * PAD, KEYS), F32),
        V((3 * PAD, KEYS), BF),
        V((3 * PAD, 128), F32),
        V((3 * PAD, 256), F32),
        V((3 * PAD, 128), F32),
        V((128, 3 * PAD), BF),
        V((128, KEYS), F32),
        V((KEYS, 128), BF),
        V((KEYS, 128), BF),
        V((8 * PAD, 128), BF),
        V((8 * PAD, 128), BF),
        V((16 * PAD, 128), BF),
        V((4, 2 * PAD, INNER), BF),
        V((4, 4, 4, 16, D), BF),
    ]
    scratch += [V((3, 4, 4, 16, w), BF) for w in widths]
    scratch += [V((4, 4, 16, w), BF) for w in widths]
    scratch += [V((3, 4, 16, w), BF) for w in widths]
    scratch += [V((4, 16, w), BF) for w in widths]
    scratch += [V((3, 16, w), BF) for w in widths]
    scratch += [
        V((2, 2, 8, D), F32),
        pltpu.SemaphoreType.DMA((8,)),
        pltpu.SemaphoreType.DMA((9,)),
        pltpu.SemaphoreType.DMA((9,)),
        pltpu.SemaphoreType.DMA((9,)),
        pltpu.SemaphoreType.DMA((9,)),
    ]
    att, ing, wq, wo = pl.pallas_call(
        kernel,
        out_shape=(
            jax.ShapeDtypeStruct((1, TOK, D), BF),
            jax.ShapeDtypeStruct((1, TOK, D), BF),
            jax.ShapeDtypeStruct((8, 3 * INNER), F32),
            jax.ShapeDtypeStruct((8, INNER), F32),
        ),
        in_specs=[any_spec] * 4,
        out_specs=(vmem,) * 4,
        scratch_shapes=scratch,
        compiler_params=pltpu.CompilerParams(
            collective_id=0, has_side_effects=True, vmem_limit_bytes=56 * 1024 * 1024),
        name="attention_sublayer",
    )(activations, qkv_weight, out_weight, out_grad)
    return att, ing, wq, wo.T


def solution(mesh):
    return jax.shard_map(
        shards,
        mesh=mesh,
        in_specs=(P("dp", "seq", None), P(), P(), P("dp", "seq", None)),
        out_specs=(
            P("dp", "seq", None),
            P("dp", "seq", None),
            P(("dp", "seq"), None),
            P(None, ("dp", "seq")),
        ),
        check_vma=False,
    )
```

time: 1710 us -> 96.2 us (0.06); the launches traced: 1680 us -> 95.9 us
  waiting for transfers between devices: 1390 us -> 0 us
  local copies, waits for them, and re-layouts: 187 us -> 6.11 us
  Pallas kernels: 0 us -> 89.1 us
  between operations: 35.1 us -> 0.64 us
  matrix products: 32.8 us -> 0 us
  loops' own time: 21.7 us -> 0 us
    unnamed x5 -> x0, waiting for transfers between devices: 1350 us -> none
    unnamed x35 -> x4, local copies, waits for them, and re-layouts: 97.6 us -> 6.11 us
    pallas_call x0 -> x1, Pallas kernels: none -> 89.1 us  [shards(): pl.pallas_call(kernel, out_shape=(jax.ShapeDtypeStruct((1, TOK, D), BF),...]
    another operation x28 -> x0, local copies, waits for them, and re-layouts: 69 us -> none
    all_gather x1 -> x0, waiting for transfers between devices: 33 us -> none  [shards(): every_kv = lax.all_gather(own_kv, 'seq', axis=1, tiled=True)]
    dot_general x20 -> x0, matrix products: 32.8 us -> none  [the longest x2 4.94 us: score_grads(): jnp.einsum('bgqhd,bkhd->bghqk', query_heads, key_part, preferred_element_...]
    another operation x34 -> x0, loops' own time: 21.7 us -> none  [the longest x17 14.6 us: shards(): lax.cond(is_live, partial(forward_block, first_key=first_key), lambda kep...]
  transfers between devices with their start and end apart: 3 -> 0, of which waited for: 3 -> 0; matrix products, arithmetic and copies ran while one was open for 1% -> 0% of each run, Pallas kernels for 0% -> 0%
where the time goes in v1:
time: 96.2 us; the launch traced here: 95.9 us
  Pallas kernels  89.1 us (93%)
  local copies, waits for them, and re-layouts  6.11 us (6%)
    pallas_call x1, Pallas kernels, shards(): pl.pallas_call(kernel, out_shape=(jax.ShapeDtypeStruct((1, TOK, D), BF),...  89.1 us
    unnamed x4, local copies, waits for them, and re-layouts  6.11 us

profile of v1, /device:TPU:1, one launch (start us, length us, event | category | flops | bytes accessed | tf_op | source)
XLA Modules:
  0.0 95.9 jit_solution(13877427794174578451)
XLA Ops:
  0.6 89.1 %attention_sublayer.1 = (bf16[1,136,1024]{2,1,0:T(8,128)(2,1)}, bf16[1,136,1024]{2,1,0:T(8,128)(2,1)}, f32[8,1536]{1,0:T(8,128)}, f32[8,512]{1,0:T(8,128)}) custom-call(bf16[1,136,1024]{2,1,0:T(8,128)(2,1)} %act_h.1, bf16[1024,1536]{1,0:T(8,128)(2,1)} %wqkv_h.1, bf16[512,1024]{1,0:T(8,128)(2,1)} %wout_h.1, bf16[1,136,1024]{2,1,0:T(8,128)(2,1)} %og_h.1), custom_call_target="tpu_custom_call" | custom-call | tf_op jit(solution)/shard_map/attention_sublayer/pallas_call | solution.py:431
  89.8 1.7 %copy.12 = bf16[1,136,1024]{2,1,0:T(8,128)(2,1)} copy(bf16[1,136,1024]{2,1,0:T(8,128)(2,1)} %get-tuple-element.16) | data formatting | bytes 557056
  91.5 1.7 %copy.13 = bf16[1,136,1024]{2,1,0:T(8,128)(2,1)} copy(bf16[1,136,1024]{2,1,0:T(8,128)(2,1)} %get-tuple-element.17) | data formatting | bytes 557056
  93.1 1.4 %copy.14 = f32[8,1536]{1,0:T(8,128)} copy(f32[8,1536]{1,0:T(8,128)} %get-tuple-element.18) | data formatting | bytes 98304
  94.6 1.3 %copy.15 = f32[512,8]{0,1:T(8,128)} copy(f32[512,8]{0,1:T(8,128)} %bitcast.1) | data formatting | bytes 32768

commit v2 on v1

--- a/solution.py
+++ b/solution.py
@@ -27,13 +27,10 @@
 BIG = 1e30
 ONE = 15
 TWO = 16
-CHUNK = 512
 BATCHES = (
-    (0, 3 * PAD, 4608),
-    (3 * PAD, 2 * PAD, 3072),
-    (5 * PAD, PAD, 2048),
-    (6 * PAD, PAD, 1536),
-    (7 * PAD, PAD, 1024),
+    (0, 3, 4608, 2304, 22, 32),
+    (3, 2, 3072, 1536, 14, 22),
+    (5, 3, 1920, 1920, 0, 14),
 )
 ORDERS = ("xyz", "yzx", "zxy")
 COLS = ((0, 384), (384, 384), (768, 256))
@@ -74,7 +71,7 @@
            al, alT, wqkv, wout, sendkv, sendqg, kvx, qg, qx, sbuf, pbuf, macc, acc, dq,
            qgT, dkT, dkvb, sibr, resb, rqc, rkv, catb, fb,
            r1a, r1b, r1c, g1a, g1b, g1c, r2a, r2b, r2c, g2a, g2b, g2c, r3a, r3b, r3c,
-           fin, lsem, ssem, rsem, fs, fr):
+           fin, attb, ingb, wob, lsem, ssem, rsem, fs, fr, ksem, dsem):
     x = lax.axis_index("dp")
     s = lax.axis_index("seq")
     head, quarter = s // 4, s % 4
@@ -128,13 +125,16 @@
 
     own_kv = pltpu.make_async_copy(rows(sendkv, head * PAD), kvslot(s), lsem.at[4])
     own_kv.start()
+    remote(rows(sendkv, head * PAD), kvslot(s), ssem.at[3], rsem.at[3], (x, sib)).start()
 
     @pl.loop(1, 16)
     def _(k):
         to = (pos + k) % 16
-        remote(rows(sendkv, (to // 2) * PAD), kvslot(s), ssem.at[0], rsem.at[0], (x, 2 * to + core)).start()
+        remote(rows(sendkv, (to // 2) * PAD), kvslot(s), ssem.at[0], ksem.at[pos], (x, 2 * to + core)).start()
 
     cin[2].wait()
+    inputs_to_sib = remote(al.at[:, pl.ds(0, PAD)], al.at[:, pl.ds(PAD, PAD)], ssem.at[2], rsem.at[2], (x, sib))
+    inputs_to_sib.start()
     cin[3].wait()
     qp = dot(al[0, 0:PAD, :], wqkv[:, 0:INNER])
     gp = dot_nt(al[1, 0:PAD, :], wout[...])
@@ -152,9 +152,6 @@
         to = (head + k) % 8
         remote(rows(sendqg, to * PAD), rows(qg, slot * PAD), ssem.at[1], rsem.at[1], (x, 4 * to + quarter)).start()
 
-    inputs_to_sib = remote(al.at[:, pl.ds(0, PAD)], al.at[:, pl.ds(PAD, PAD)], ssem.at[2], rsem.at[2], (x, sib))
-    inputs_to_sib.start()
-
     lo, hi = lane_bounds(PAD)
     place = lax.broadcasted_iota(jnp.int32, (PAD, 128), 0)
 
@@ -164,13 +161,18 @@
         kvx[pl.ds(pl.multiple_of(g * PAD, 16), PAD), 128:256] = jnp.where(
             (t >= lo) & (t < hi), 1.0, 0.0).astype(BF)
 
+    @pl.loop(1, 16)
+    def _(k):
+        frm = (pos + 16 - k) % 16
+        g = 2 * frm + core
+        remote(kvslot(g), kvslot(g), ssem.at[0], ksem.at[frm], (x, sib)).wait_recv()
+        remote(kvslot(g), kvslot(g), ssem.at[3], rsem.at[3], (x, sib)).start()
+
     own_kv.wait()
-    remote(rows(dkvb, 0, 15 * PAD), rows(dkvb, 0, 15 * PAD), ssem.at[0], rsem.at[0], (x, sib)).wait_recv()
-
-    @pl.loop(0, 16)
-    def _(k):
-        g = 2 * k + core
-        remote(kvslot(g), kvslot(g), ssem.at[3], rsem.at[3], (x, sib)).start()
+    inputs_to_sib.wait()
+    for i in range(2):
+        for j in range(8):
+            alT[i, 128 * j:128 * j + 128, :] = al[i, :, 128 * j:128 * j + 128].T
 
     own_qg.wait()
     remote(rows(dkvb, 0, 7 * PAD), rows(dkvb, 0, 7 * PAD), ssem.at[1], rsem.at[1], (x, sib)).wait_recv()
@@ -185,14 +187,48 @@
 
     remote(rows(dkvb, 0, 16 * PAD), rows(dkvb, 0, 16 * PAD), ssem.at[3], rsem.at[3], (x, sib)).wait()
 
-    for number, (row0, count, keys) in enumerate(BATCHES):
+    part = 2 * head + (pos % 2)
+
+    def finish(lo_group, hi_group):
+        lo_row, hi_row = lo_group * PAD, hi_group * PAD
+        for blk in range(lo_row // 128, -(-hi_row // 128)):
+            a, b = max(lo_row - 128 * blk, 0), min(hi_row - 128 * blk, 128)
+            v = dkT[:, 128 * blk:128 * blk + 128].T
+            dkvb[128 * blk + a:128 * blk + b, :] = v[a:b].astype(BF)
+
+    def to_sibling(number, lo_group, hi_group):
+        @pl.loop(lo_group // 2, hi_group // 2)
+        def _(k):
+            g = 2 * k + 1 - core
+            remote(rows(dkvb, g * PAD), rows(sibr, g * PAD), ssem.at[5], dsem.at[number], (x, sib)).start()
+
+    def to_owners(number, lo_group, hi_group):
+        n = (hi_group - lo_group) // 2 * PAD
+        remote(rows(dkvb, 0, n), rows(sibr, 0, n), ssem.at[5], dsem.at[number], (x, sib)).wait_recv()
+
+        @pl.loop(lo_group // 2, hi_group // 2)
+        def _(k):
+            g = 2 * k + core
+            r = pl.ds(pl.multiple_of(g * PAD, 16), PAD)
+            dkvb[r, :] = (dkvb[r, :].astype(F32) + sibr[r, :].astype(F32)).astype(BF)
+
+            @pl.when(k != pos)
+            def _():
+                remote(rows(dkvb, g * PAD), rows(rkv, part * PAD), ssem.at[6], rsem.at[6], (x, g)).start()
+
+            @pl.when(k == pos)
+            def _():
+                pltpu.make_async_copy(rows(dkvb, g * PAD), rows(rkv, part * PAD), lsem.at[7]).start()
+
+    for number, (slot0, slots, keys, CHUNK, lo_group, hi_group) in enumerate(BATCHES):
+        row0, count = slot0 * PAD, slots * PAD
         rr = slice(row0, row0 + count)
         steps = keys // CHUNK
         macc[0:count, :] = jnp.full((count, 128), -3e38, F32)
 
         @pl.loop(0, steps)
         def _(c):
-            kk = pl.ds(pl.multiple_of(c * CHUNK, CHUNK), CHUNK)
+            kk = pl.ds(pl.multiple_of(c * CHUNK, 128), CHUNK)
             sc = dot_nt(qx[rr, :], kvx[kk, :])
             sbuf[0:count, kk] = sc
             top = macc[0:count, :]
@@ -205,7 +241,7 @@
 
         @pl.loop(0, steps)
         def _(c):
-            kk = pl.ds(pl.multiple_of(c * CHUNK, CHUNK), CHUNK)
+            kk = pl.ds(pl.multiple_of(c * CHUNK, 128), CHUNK)
             p = jnp.exp(sbuf[0:count, kk] - row_max).astype(BF)
             pbuf[0:count, kk] = p
             acc[0:count, :] += dot(p, kvx[kk, :])
@@ -226,7 +262,7 @@
 
         @pl.loop(0, steps)
         def _(c):
-            kk = pl.ds(pl.multiple_of(c * CHUNK, CHUNK), CHUNK)
+            kk = pl.ds(pl.multiple_of(c * CHUNK, 128), CHUNK)
             p = pbuf[0:count, kk]
             dpd = dot_nt(qx[rr, :], kvx[kk, :])
             ds = (p.astype(F32) * dpd).astype(BF)
@@ -242,47 +278,26 @@
 
         resb[rr, :] = jnp.where(near, dq[0:count, :] * (0.125 * inv), ctx.astype(F32)).astype(BF)
 
-    own_res = pltpu.make_async_copy(rows(resb, slot * PAD), rows(rqc, head * PAD), lsem.at[6])
-    own_res.start()
-
-    @pl.loop(1, 8)
-    def _(k):
-        to = (head + k) % 8
-        remote(rows(resb, (7 - to) * PAD), rows(rqc, head * PAD), ssem.at[4], rsem.at[4],
-               (x, 4 * to + quarter)).start()
-
-    @pl.loop(0, KEYS // CHUNK)
-    def _(c):
-        kk = pl.ds(pl.multiple_of(c * CHUNK, CHUNK), CHUNK)
-        dkvb[kk, :] = dkT[:, kk].T.astype(BF)
-
-    @pl.loop(0, 16)
-    def _(k):
-        g = 2 * k + 1 - core
-        remote(rows(dkvb, g * PAD), rows(sibr, g * PAD), ssem.at[5], rsem.at[5], (x, sib)).start()
-
-    remote(rows(dkvb, 0, 16 * PAD), rows(sibr, 0, 16 * PAD), ssem.at[5], rsem.at[5], (x, sib)).wait_recv()
-
-    @pl.loop(0, 16)
-    def _(k):
-        r = pl.ds(pl.multiple_of((2 * k + core) * PAD, 16), PAD)
-        dkvb[r, :] = (dkvb[r, :].astype(F32) + sibr[r, :].astype(F32)).astype(BF)
-
-    part = 2 * head + (pos % 2)
-    own_dkv = pltpu.make_async_copy(rows(dkvb, s * PAD), rows(rkv, part * PAD), lsem.at[7])
-    own_dkv.start()
-
-    @pl.loop(1, 16)
-    def _(k):
-        to = 2 * ((pos + k) % 16) + core
-        remote(rows(dkvb, to * PAD), rows(rkv, part * PAD), ssem.at[6], rsem.at[6], (x, to)).start()
-
-    inputs_to_sib.wait()
-    for i in range(2):
-        for j in range(8):
-            alT[i, 128 * j:128 * j + 128, :] = al[i, :, 128 * j:128 * j + 128].T
-
-    own_res.wait()
+        for j in range(slot0, slot0 + slots):
+            to = 7 - j
+
+            @pl.when(head != to)
+            def _():
+                remote(rows(resb, j * PAD), rows(rqc, head * PAD), ssem.at[4], rsem.at[4],
+                       (x, 4 * to + quarter)).start()
+
+            @pl.when(head == to)
+            def _():
+                pltpu.make_async_copy(rows(resb, j * PAD), rows(rqc, head * PAD), lsem.at[6]).start()
+
+        finish(lo_group, hi_group)
+        to_sibling(number, lo_group, hi_group)
+        if number > 0:
+            to_owners(number - 1, *BATCHES[number - 1][4:])
+
+    to_owners(len(BATCHES) - 1, *BATCHES[-1][4:])
+
+    pltpu.make_async_copy(rows(resb, 0), rows(rqc, 0), lsem.at[6]).wait()
     remote(rows(rqc, 0, 7 * PAD), rows(rqc, 0, 7 * PAD), ssem.at[4], rsem.at[4], (x, sib)).wait()
     for i in range(4):
         a = rqc[(2 * i) * PAD:(2 * i + 1) * PAD, :].astype(F32)
@@ -291,9 +306,16 @@
         catb[0, 0:PAD, 128 * i:128 * i + 128] = q_pair.astype(BF)
         catb[3, 0:PAD, 128 * i:128 * i + 128] = c_pair.astype(BF)
     att = dot(catb[3, 0:PAD, :], wout[...])
-    att_o[0] = att[0:TOK].astype(BF)
-
-    own_dkv.wait()
+    attb[...] = att[0:TOK].astype(BF)
+    outs = [
+        pltpu.make_async_copy(attb, att_o.at[0], lsem.at[0]),
+        pltpu.make_async_copy(ingb, ing_o.at[0], lsem.at[1]),
+        pltpu.make_async_copy(wob.at[:, pl.ds(0, 3 * INNER)], wq_o, lsem.at[2]),
+        pltpu.make_async_copy(wob.at[:, pl.ds(3 * INNER, INNER)], wo_o, lsem.at[3]),
+    ]
+    outs[0].start()
+
+    pltpu.make_async_copy(rows(dkvb, 0), rows(rkv, 0), lsem.at[7]).wait()
     remote(rows(rkv, 0, 15 * PAD), rows(rkv, 0, 15 * PAD), ssem.at[6], rsem.at[6], (x, sib)).wait()
     for i in range(4):
         a = rkv[(4 * i) * PAD:(4 * i + 1) * PAD, :].astype(F32) + rkv[(4 * i + 1) * PAD:(4 * i + 2) * PAD, :].astype(F32)
@@ -308,7 +330,8 @@
     ing = dot_nt(catb[0, 0:PAD, :], wqkv[:, 0:INNER])
     ing += dot_nt(catb[1, 0:PAD, :], wqkv[:, INNER:2 * INNER])
     ing += dot_nt(catb[2, 0:PAD, :], wqkv[:, 2 * INNER:])
-    ing_o[0] = ing[0:TOK].astype(BF)
+    ingb[...] = ing[0:TOK].astype(BF)
+    outs[1].start()
     cat_to_sib.wait()
 
     for half in range(2):
@@ -376,18 +399,29 @@
     last = remote(fin.at[core, 1 - core], fin.at[core, 1 - core], ssem.at[8], rsem.at[8], (x, sib))
     last.start()
     last.wait()
-    wq_o[:, 0:D] = fin[0, core]
-    wq_o[:, D:] = fin[1, core, :, 0:INNER]
-    wo_o[...] = fin[1, core, :, INNER:]
+    wob[:, 0:D] = fin[0, core]
+    wob[:, D:] = fin[1, core]
+    outs[2].start()
+    outs[3].start()
 
     remote(rows(dkvb, 0, 15 * PAD), rows(dkvb, 0, 15 * PAD), ssem.at[0], rsem.at[0], (x, sib)).wait_send()
     remote(rows(dkvb, 0, 7 * PAD), rows(dkvb, 0, 7 * PAD), ssem.at[1], rsem.at[1], (x, sib)).wait_send()
     remote(rows(dkvb, 0, 16 * PAD), rows(dkvb, 0, 16 * PAD), ssem.at[5], rsem.at[5], (x, sib)).wait_send()
+    for c in outs:
+        c.wait()
+
+
+def hand_out(*refs):
+    sems = refs[8]
+    copies = [pltpu.make_async_copy(refs[i], refs[4 + i], sems.at[i]) for i in range(4)]
+    for c in copies:
+        c.start()
+    for c in copies:
+        c.wait()
 
 
 def shards(activations, qkv_weight, out_weight, out_grad):
     any_spec = pl.BlockSpec(memory_space=pl.ANY)
-    vmem = pl.BlockSpec(memory_space=pltpu.VMEM)
     V = pltpu.VMEM
     widths = [c[1] for c in COLS]
     scratch = [
@@ -422,13 +456,18 @@
     scratch += [V((3, 16, w), BF) for w in widths]
     scratch += [
         V((2, 2, 8, D), F32),
+        V((TOK, D), BF),
+        V((TOK, D), BF),
+        V((8, 2 * D), F32),
         pltpu.SemaphoreType.DMA((8,)),
         pltpu.SemaphoreType.DMA((9,)),
         pltpu.SemaphoreType.DMA((9,)),
         pltpu.SemaphoreType.DMA((9,)),
         pltpu.SemaphoreType.DMA((9,)),
+        pltpu.SemaphoreType.DMA((16,)),
+        pltpu.SemaphoreType.DMA((3,)),
     ]
-    att, ing, wq, wo = pl.pallas_call(
+    made = pl.pallas_call(
         kernel,
         out_shape=(
             jax.ShapeDtypeStruct((1, TOK, D), BF),
@@ -437,12 +476,20 @@
             jax.ShapeDtypeStruct((8, INNER), F32),
         ),
         in_specs=[any_spec] * 4,
-        out_specs=(vmem,) * 4,
+        out_specs=(any_spec,) * 4,
         scratch_shapes=scratch,
         compiler_params=pltpu.CompilerParams(
             collective_id=0, has_side_effects=True, vmem_limit_bytes=56 * 1024 * 1024),
         name="attention_sublayer",
     )(activations, qkv_weight, out_weight, out_grad)
+    att, ing, wq, wo = pl.pallas_call(
+        hand_out,
+        out_shape=tuple(jax.ShapeDtypeStruct(a.shape, a.dtype) for a in made),
+        in_specs=[any_spec] * 4,
+        out_specs=(any_spec,) * 4,
+        scratch_shapes=[pltpu.SemaphoreType.DMA((4,))],
+        name="hand_out",
+    )(*made)
     return att, ing, wq, wo.T
 
 

time: 96.2 us -> 97.4 us (1.012)
  Pallas kernels: 89.1 us -> 96.7 us
  local copies, waits for them, and re-layouts: 6.11 us -> 0 us
    pallas_call x0 -> x1, Pallas kernels: none -> 20 us  [shards(): pl.pallas_call(hand_out, out_shape=tuple((jax.ShapeDtypeStruct(a.shape, a...]
    pallas_call x1, Pallas kernels: 89.1 us -> 76.7 us  [shards(): pl.pallas_call(kernel, out_shape=(jax.ShapeDtypeStruct((1, TOK, D), BF),...]
    unnamed x4 -> x0, local copies, waits for them, and re-layouts: 6.11 us -> none
where the time goes in v2:
time: 97.4 us; the launch traced here: 97.3 us
  Pallas kernels  96.7 us (99%)
    pallas_call x1, Pallas kernels, shards(): pl.pallas_call(kernel, out_shape=(jax.ShapeDtypeStruct((1, TOK, D), BF),...  76.7 us
    pallas_call x1, Pallas kernels, shards(): pl.pallas_call(hand_out, out_shape=tuple((jax.ShapeDtypeStruct(a.shape, a...  20 us

profile of v2, /device:TPU:1, one launch (start us, length us, event | category | flops | bytes accessed | tf_op | source)
XLA Modules:
  0.0 97.3 jit_solution(13708398169157209576)
XLA Ops:
  0.6 76.7 %attention_sublayer.1 = (bf16[1,136,1024]{2,1,0:T(8,128)(2,1)}, bf16[1,136,1024]{2,1,0:T(8,128)(2,1)}, f32[8,1536]{1,0:T(8,128)}, f32[8,512]{1,0:T(8,128)}) custom-call(bf16[1,136,1024]{2,1,0:T(8,128)(2,1)} %act_h.1, bf16[1024,1536]{1,0:T(8,128)(2,1)} %wqkv_h.1, bf16[512,1024]{1,0:T(8,128)(2,1)} %wout_h.1, bf16[1,136,1024]{2,1,0:T(8,128)(2,1)} %og_h.1), custom_call_target="tpu_custom_call" | custom-call | tf_op jit(solution)/shard_map/attention_sublayer/pallas_call | solution.py:470
  77.3 20.0 %hand_out.1 = (bf16[1,136,1024]{2,1,0:T(8,128)(2,1)}, bf16[1,136,1024]{2,1,0:T(8,128)(2,1)}, f32[8,1536]{1,0:T(8,128)}, f32[8,512]{1,0:T(8,128)}) custom-call(bf16[1,136,1024]{2,1,0:T(8,128)(2,1)} %get-tuple-element.12.refs_0_, bf16[1,136,1024]{2,1,0:T(8,128)(2,1)} %get-tuple-element.13.refs_1_, f32[8,1536]{1,0:T(8,128)} %get-tuple-element.14.refs_2_, ...), custom_call_target="tpu_custom_call" | custom-call | tf_op jit(solution)/shard_map/hand_out/pallas_call | solution.py:485

commit v3 on v2

--- a/solution.py
+++ b/solution.py
@@ -412,11 +412,15 @@
 
 
 def hand_out(*refs):
-    sems = refs[8]
-    copies = [pltpu.make_async_copy(refs[i], refs[4 + i], sems.at[i]) for i in range(4)]
-    for c in copies:
+    came, gone, held, sems = refs[0:4], refs[4:8], refs[8:12], refs[12]
+    ins = [pltpu.make_async_copy(came[i], held[i], sems.at[i]) for i in range(4)]
+    outs = [pltpu.make_async_copy(held[i], gone[i], sems.at[4 + i]) for i in range(4)]
+    for c in ins:
         c.start()
-    for c in copies:
+    for i in range(4):
+        ins[i].wait()
+        outs[i].start()
+    for c in outs:
         c.wait()
 
 
@@ -487,7 +491,7 @@
         out_shape=tuple(jax.ShapeDtypeStruct(a.shape, a.dtype) for a in made),
         in_specs=[any_spec] * 4,
         out_specs=(any_spec,) * 4,
-        scratch_shapes=[pltpu.SemaphoreType.DMA((4,))],
+        scratch_shapes=[V(a.shape, a.dtype) for a in made] + [pltpu.SemaphoreType.DMA((8,))],
         name="hand_out",
     )(*made)
     return att, ing, wq, wo.T

time: 97.4 us -> 79.3 us (0.81)
  Pallas kernels: 96.7 us -> 78.5 us
    pallas_call x1, Pallas kernels: 20 us -> 1.83 us  [shards(): pl.pallas_call(hand_out, out_shape=tuple((jax.ShapeDtypeStruct(a.shape, a...]
where the time goes in v3:
time: 79.3 us; the launch traced here: 79.2 us
  Pallas kernels  78.5 us (99%)
    pallas_call x1, Pallas kernels, shards(): pl.pallas_call(kernel, out_shape=(jax.ShapeDtypeStruct((1, TOK, D), BF),...  76.7 us
    pallas_call x1, Pallas kernels, shards(): pl.pallas_call(hand_out, out_shape=tuple((jax.ShapeDtypeStruct(a.shape, a...  1.83 us

profile of v3, /device:TPU:1, one launch (start us, length us, event | category | flops | bytes accessed | tf_op | source)
XLA Modules:
  0.0 79.2 jit_solution(1056886030007486553)
XLA Ops:
  0.6 76.7 %attention_sublayer.1 = (bf16[1,136,1024]{2,1,0:T(8,128)(2,1)}, bf16[1,136,1024]{2,1,0:T(8,128)(2,1)}, f32[8,1536]{1,0:T(8,128)}, f32[8,512]{1,0:T(8,128)}) custom-call(bf16[1,136,1024]{2,1,0:T(8,128)(2,1)} %act_h.1, bf16[1024,1536]{1,0:T(8,128)(2,1)} %wqkv_h.1, bf16[512,1024]{1,0:T(8,128)(2,1)} %wout_h.1, bf16[1,136,1024]{2,1,0:T(8,128)(2,1)} %og_h.1), custom_call_target="tpu_custom_call" | custom-call | tf_op jit(solution)/shard_map/attention_sublayer/pallas_call | solution.py:474
  77.3 1.8 %hand_out.1 = (bf16[1,136,1024]{2,1,0:T(8,128)(2,1)}, bf16[1,136,1024]{2,1,0:T(8,128)(2,1)}, f32[8,1536]{1,0:T(8,128)}, f32[8,512]{1,0:T(8,128)}) custom-call(bf16[1,136,1024]{2,1,0:T(8,128)(2,1)} %get-tuple-element.12.refs_0_, bf16[1,136,1024]{2,1,0:T(8,128)(2,1)} %get-tuple-element.13.refs_1_, f32[8,1536]{1,0:T(8,128)} %get-tuple-element.14.refs_2_, ...), custom_call_target="tpu_custom_call" | custom-call | tf_op jit(solution)/shard_map/hand_out/pallas_call | solution.py:489

commit v4 on v3

--- a/solution.py
+++ b/solution.py
@@ -32,8 +32,6 @@
     (3, 2, 3072, 1536, 14, 22),
     (5, 3, 1920, 1920, 0, 14),
 )
-ORDERS = ("xyz", "yzx", "zxy")
-COLS = ((0, 384), (384, 384), (768, 256))
 NT = (((1,), (1,)), ((), ()))
 
 
@@ -69,20 +67,19 @@
 
 def kernel(act_h, wqkv_h, wout_h, og_h, att_o, ing_o, wq_o, wo_o,
            al, alT, wqkv, wout, sendkv, sendqg, kvx, qg, qx, sbuf, pbuf, macc, acc, dq,
-           qgT, dkT, dkvb, sibr, resb, rqc, rkv, catb, fb,
-           r1a, r1b, r1c, g1a, g1b, g1c, r2a, r2b, r2c, g2a, g2b, g2c, r3a, r3b, r3c,
-           fin, attb, ingb, wob, lsem, ssem, rsem, fs, fr, ksem, dsem):
+           qgT, dkT, dkvb, sibr, resb, rqc, rkv, catp, cgx, fb, fr, fo, fi,
+           attb, ingb, wob, lsem, ssem, rsem, ksem, dsem, xsem):
     x = lax.axis_index("dp")
     s = lax.axis_index("seq")
     head, quarter = s // 4, s % 4
     pos, core = s // 2, s % 2
-    y, z = s // 8, (s // 2) % 4
     sib = s + 1 - 2 * core
+    spot = 2 * x + core
 
     cin = [
-        pltpu.make_async_copy(act_h.at[0], al.at[0, pl.ds(0, TOK)], lsem.at[0]),
+        pltpu.make_async_copy(act_h.at[0], al.at[0, spot, pl.ds(0, TOK)], lsem.at[0]),
         pltpu.make_async_copy(wqkv_h, wqkv, lsem.at[1]),
-        pltpu.make_async_copy(og_h.at[0], al.at[1, pl.ds(0, TOK)], lsem.at[2]),
+        pltpu.make_async_copy(og_h.at[0], al.at[1, spot, pl.ds(0, TOK)], lsem.at[2]),
         pltpu.make_async_copy(wout_h, wout, lsem.at[3]),
     ]
     for c in cin:
@@ -94,13 +91,15 @@
     def _(k):
         pl.semaphore_signal(bar, inc=1, device_id=(x, 2 * ((pos + k) % 16) + core), device_id_type=MESH)
 
-    pl.semaphore_signal(bar, inc=1, device_id=(x, sib), device_id_type=MESH)
-    for k in range(1, 4):
-        pl.semaphore_signal(bar, inc=1, device_id=((x + k) % 4, s), device_id_type=MESH)
-
-    al[0, TOK:PAD, :] = jnp.zeros((PAD - TOK, D), BF)
-    al[1, TOK:PAD, :] = jnp.zeros((PAD - TOK, D), BF)
-    pl.semaphore_wait(bar, 19)
+    def at_spot(q):
+        return (q // 2, 2 * pos + q % 2)
+
+    @pl.loop(1, 8)
+    def _(k):
+        pl.semaphore_signal(bar, inc=1, device_id=at_spot((spot + k) % 8), device_id_type=MESH)
+
+    for i in range(2):
+        al[i, spot, TOK:PAD, :] = jnp.zeros((PAD - TOK, D), BF)
 
     def remote(src, dst, send, recv, dev):
         return pltpu.make_async_remote_copy(
@@ -116,13 +115,14 @@
 
     cin[0].wait()
     cin[1].wait()
-    kp = dot(al[0, 0:PAD, :], wqkv[:, INNER:2 * INNER])
-    vp = dot(al[0, 0:PAD, :], wqkv[:, 2 * INNER:])
+    kp = dot(al[0, spot], wqkv[:, INNER:2 * INNER])
+    vp = dot(al[0, spot], wqkv[:, 2 * INNER:])
     for i in range(4):
         a, b = swap_pack(kp[:, 128 * i:128 * i + 128], vp[:, 128 * i:128 * i + 128], left)
         sendkv[(2 * i) * PAD:(2 * i + 1) * PAD, :] = a.astype(BF)
         sendkv[(2 * i + 1) * PAD:(2 * i + 2) * PAD, :] = b.astype(BF)
 
+    pl.semaphore_wait(bar, 22)
     own_kv = pltpu.make_async_copy(rows(sendkv, head * PAD), kvslot(s), lsem.at[4])
     own_kv.start()
     remote(rows(sendkv, head * PAD), kvslot(s), ssem.at[3], rsem.at[3], (x, sib)).start()
@@ -133,15 +133,19 @@
         remote(rows(sendkv, (to // 2) * PAD), kvslot(s), ssem.at[0], ksem.at[pos], (x, 2 * to + core)).start()
 
     cin[2].wait()
-    inputs_to_sib = remote(al.at[:, pl.ds(0, PAD)], al.at[:, pl.ds(PAD, PAD)], ssem.at[2], rsem.at[2], (x, sib))
-    inputs_to_sib.start()
     cin[3].wait()
-    qp = dot(al[0, 0:PAD, :], wqkv[:, 0:INNER])
-    gp = dot_nt(al[1, 0:PAD, :], wout[...])
+    qp = dot(al[0, spot], wqkv[:, 0:INNER])
+    gp = dot_nt(al[1, spot], wout[...])
     for i in range(4):
         a, b = swap_pack(qp[:, 128 * i:128 * i + 128], gp[:, 128 * i:128 * i + 128], left)
         sendqg[(2 * i) * PAD:(2 * i + 1) * PAD, :] = a.astype(BF)
         sendqg[(2 * i + 1) * PAD:(2 * i + 2) * PAD, :] = b.astype(BF)
+
+    @pl.loop(1, 4)
+    def _(k):
+        remote(al.at[:, spot], al.at[:, spot], ssem.at[2], xsem.at[x], ((x + k) % 4, s)).start()
+
+    remote(al.at[:, spot], al.at[:, spot], ssem.at[7], rsem.at[7], (x, sib)).start()
 
     slot = 7 - s // 4
     own_qg = pltpu.make_async_copy(rows(sendqg, head * PAD), rows(qg, slot * PAD), lsem.at[5])
@@ -169,11 +173,6 @@
         remote(kvslot(g), kvslot(g), ssem.at[3], rsem.at[3], (x, sib)).start()
 
     own_kv.wait()
-    inputs_to_sib.wait()
-    for i in range(2):
-        for j in range(8):
-            alT[i, 128 * j:128 * j + 128, :] = al[i, :, 128 * j:128 * j + 128].T
-
     own_qg.wait()
     remote(rows(dkvb, 0, 7 * PAD), rows(dkvb, 0, 7 * PAD), ssem.at[1], rsem.at[1], (x, sib)).wait_recv()
 
@@ -236,6 +235,8 @@
                 top = jnp.maximum(top, sc[:, 128 * i:128 * i + 128])
             macc[0:count, :] = top
 
+        if number > 0:
+            to_owners(number - 1, *BATCHES[number - 1][4:])
         row_max = jnp.max(macc[0:count, :], axis=1, keepdims=True)
         acc[0:count, :] = jnp.zeros((count, 256), F32)
 
@@ -292,8 +293,25 @@
 
         finish(lo_group, hi_group)
         to_sibling(number, lo_group, hi_group)
-        if number > 0:
-            to_owners(number - 1, *BATCHES[number - 1][4:])
+        if number == 1:
+            @pl.loop(1, 4)
+            def _(k):
+                frm = (x + k) % 4
+                q = 2 * frm + core
+                remote(al.at[:, q], al.at[:, q], ssem.at[2], xsem.at[frm], (x, sib)).wait_recv()
+                remote(al.at[:, q], al.at[:, q], ssem.at[7], rsem.at[7], (x, sib)).start()
+
+    remote(al.at[:, pl.ds(0, 4)], al.at[:, pl.ds(0, 4)], ssem.at[7], rsem.at[7], (x, sib)).wait()
+
+    def transpose_inputs(i):
+        for j in range(8):
+            alT[i, 128 * j:128 * j + 128, :] = al[i, :, :, 128 * j:128 * j + 128].reshape(8 * PAD, 128).T
+
+    transpose_inputs(0)
+
+    @pl.when(core == 1)
+    def _():
+        transpose_inputs(1)
 
     to_owners(len(BATCHES) - 1, *BATCHES[-1][4:])
 
@@ -303,9 +321,49 @@
         a = rqc[(2 * i) * PAD:(2 * i + 1) * PAD, :].astype(F32)
         b = rqc[(2 * i + 1) * PAD:(2 * i + 2) * PAD, :].astype(F32)
         q_pair, c_pair = swap_pack(a, b, left)
-        catb[0, 0:PAD, 128 * i:128 * i + 128] = q_pair.astype(BF)
-        catb[3, 0:PAD, 128 * i:128 * i + 128] = c_pair.astype(BF)
-    att = dot(catb[3, 0:PAD, :], wout[...])
+        catp[0, i] = q_pair.astype(BF)
+        catp[3, i] = c_pair.astype(BF)
+
+    def wide(i):
+        return jnp.concatenate([catp[i, j] for j in range(4)], axis=1)
+
+    def exchange(u, blocks):
+        own = pltpu.make_async_copy(catp.at[blocks[0] + (blocks[1] - blocks[0]) * core, x], cgx.at[u, spot], lsem.at[4 + u])
+        own.start()
+
+        @pl.loop(1, 8)
+        def _(k):
+            q = (spot + k) % 8
+            block = blocks[0] + (blocks[1] - blocks[0]) * (q % 2)
+            remote(catp.at[block, q // 2], cgx.at[u, spot], ssem.at[8 + u], rsem.at[8 + u], at_spot(q)).start()
+
+        return own
+
+    def partial_sums(u, own, lhs):
+        own.wait()
+        seven = cgx.at[u, pl.ds(0, 7)]
+        remote(seven, seven, ssem.at[8 + u], rsem.at[8 + u], (x, sib)).wait()
+        right = cgx[u].reshape(8 * PAD, 128)
+        for i in range(4):
+            f = dot(alT[lhs, 256 * i:256 * i + 256, :], right)
+            fb[u, :, i] = f.astype(BF).reshape(16, 16, 128)
+
+        @pl.loop(1, 16)
+        def _(k):
+            to = (pos + k) % 16
+            remote(fb.at[u, to], fr.at[u, k - 1], ssem.at[10 + u], rsem.at[10 + u], (x, 2 * to + core)).start()
+
+    def sums(u):
+        remote(fr.at[u], fr.at[u], ssem.at[10 + u], rsem.at[10 + u], (x, sib)).wait()
+        v = fb[u, pos].astype(F32)
+        for k in range(15):
+            v += fr[u, k].astype(F32)
+        for i in range(4):
+            for c in range(2):
+                fo[2 * i + c, u] = v[i, 8 * c:8 * c + 8]
+
+    early = exchange(0, (0, 3))
+    att = dot(wide(3), wout[...])
     attb[...] = att[0:TOK].astype(BF)
     outs = [
         pltpu.make_async_copy(attb, att_o.at[0], lsem.at[0]),
@@ -314,6 +372,7 @@
         pltpu.make_async_copy(wob.at[:, pl.ds(3 * INNER, INNER)], wo_o, lsem.at[3]),
     ]
     outs[0].start()
+    partial_sums(0, early, core)
 
     pltpu.make_async_copy(rows(dkvb, 0), rows(rkv, 0), lsem.at[7]).wait()
     remote(rows(rkv, 0, 15 * PAD), rows(rkv, 0, 15 * PAD), ssem.at[6], rsem.at[6], (x, sib)).wait()
@@ -321,92 +380,37 @@
         a = rkv[(4 * i) * PAD:(4 * i + 1) * PAD, :].astype(F32) + rkv[(4 * i + 1) * PAD:(4 * i + 2) * PAD, :].astype(F32)
         b = rkv[(4 * i + 2) * PAD:(4 * i + 3) * PAD, :].astype(F32) + rkv[(4 * i + 3) * PAD:(4 * i + 4) * PAD, :].astype(F32)
         k_pair, v_pair = swap_pack(a, b, left)
-        catb[1, 0:PAD, 128 * i:128 * i + 128] = k_pair.astype(BF)
-        catb[2, 0:PAD, 128 * i:128 * i + 128] = v_pair.astype(BF)
-
-    cat_to_sib = remote(catb.at[pl.ds(2 - 2 * core, 2), pl.ds(0, PAD)], catb.at[pl.ds(2 - 2 * core, 2), pl.ds(PAD, PAD)],
-                        ssem.at[7], rsem.at[7], (x, sib))
-    cat_to_sib.start()
-    ing = dot_nt(catb[0, 0:PAD, :], wqkv[:, 0:INNER])
-    ing += dot_nt(catb[1, 0:PAD, :], wqkv[:, INNER:2 * INNER])
-    ing += dot_nt(catb[2, 0:PAD, :], wqkv[:, 2 * INNER:])
+        catp[1, i] = k_pair.astype(BF)
+        catp[2, i] = v_pair.astype(BF)
+
+    late = exchange(1, (1, 2))
+    ing = dot_nt(wide(0), wqkv[:, 0:INNER])
+    ing += dot_nt(wide(1), wqkv[:, INNER:2 * INNER])
+    ing += dot_nt(wide(2), wqkv[:, 2 * INNER:])
     ingb[...] = ing[0:TOK].astype(BF)
     outs[1].start()
-    cat_to_sib.wait()
-
-    for half in range(2):
-        which = 0 if half == 0 else core
-        right = catb[2 * core + half]
-
-        @pl.loop(0, 4)
-        def _(i):
-            f = dot(alT[which, pl.ds(pl.multiple_of(i * 256, 256), 256), :], right)
-            fb[i, :, :, :, INNER * half:INNER * half + INNER] = f.astype(BF).reshape(4, 4, 16, INNER)
-
-    coords = {"x": x, "y": y, "z": z}
-
-    def peer(axis, k):
-        c = dict(coords)
-        c[axis] = (coords[axis] + k) % 4
-        return c[axis], (c["x"], c["y"] * 8 + c["z"] * 2 + core)
-
-    def stage(o, phase, take, recv):
-        for k in range(1, 4):
-            there, dev = peer(ORDERS[o][phase], k)
-            remote(take(there), recv.at[k - 1], fs.at[3 * phase + o], fr.at[3 * phase + o], dev).start()
-
-    def arrived(o, phase, recv):
-        remote(recv, recv, fs.at[3 * phase + o], fr.at[3 * phase + o], (x, sib)).wait()
-
-    def total(mine, recv):
-        v = mine.astype(F32)
-        for k in range(3):
-            v += recv[k].astype(F32)
-        return v
-
-    def cols(o):
-        return pl.ds(*COLS[o])
-
-    takes1 = (
-        lambda t: fb.at[t, :, :, :, cols(0)],
-        lambda t: fb.at[:, t, :, :, cols(1)],
-        lambda t: fb.at[:, :, t, :, cols(2)],
-    )
-    r1, g1 = (r1a, r1b, r1c), (g1a, g1b, g1c)
-    r2, g2 = (r2a, r2b, r2c), (g2a, g2b, g2c)
-    r3 = (r3a, r3b, r3c)
-    takes2 = (lambda t: g1a.at[t], lambda t: g1b.at[:, t], lambda t: g1c.at[t])
-    for o in range(3):
-        stage(o, 0, takes1[o], r1[o])
-    for o in range(3):
-        arrived(o, 0, r1[o])
-        mine = coords[ORDERS[o][0]]
-        g1[o][...] = total(takes1[o](mine)[...], r1[o]).astype(BF)
-        stage(o, 1, takes2[o], r2[o])
-    for o in range(3):
-        arrived(o, 1, r2[o])
-        mine = coords[ORDERS[o][1]]
-        g2[o][...] = total(takes2[o](mine)[...], r2[o]).astype(BF)
-        stage(o, 2, lambda t, o=o: g2[o].at[t], r3[o])
-    for o in range(3):
-        arrived(o, 2, r3[o])
-        mine = coords[ORDERS[o][2]]
-        v = total(g2[o][mine], r3[o])
-        a, n = COLS[o]
-        fin[core, 0, :, a:a + n] = v[0:8]
-        fin[core, 1, :, a:a + n] = v[8:16]
-
-    last = remote(fin.at[core, 1 - core], fin.at[core, 1 - core], ssem.at[8], rsem.at[8], (x, sib))
-    last.start()
-    last.wait()
-    wob[:, 0:D] = fin[0, core]
-    wob[:, D:] = fin[1, core]
+    partial_sums(1, late, 0)
+    sums(0)
+    sums(1)
+
+    fi[spot] = fo[spot]
+
+    @pl.loop(1, 8)
+    def _(k):
+        q = (spot + k) % 8
+        remote(fo.at[q], fi.at[spot], ssem.at[12], rsem.at[12], at_spot(q)).start()
+
+    remote(fi.at[pl.ds(0, 7)], fi.at[pl.ds(0, 7)], ssem.at[12], rsem.at[12], (x, sib)).wait()
+    for i in range(4):
+        for block, (c, u) in enumerate(((0, 0), (0, 1), (1, 1), (1, 0))):
+            wob[:, INNER * block + 128 * i:INNER * block + 128 * i + 128] = fi[2 * i + c, u]
     outs[2].start()
     outs[3].start()
 
     remote(rows(dkvb, 0, 15 * PAD), rows(dkvb, 0, 15 * PAD), ssem.at[0], rsem.at[0], (x, sib)).wait_send()
     remote(rows(dkvb, 0, 7 * PAD), rows(dkvb, 0, 7 * PAD), ssem.at[1], rsem.at[1], (x, sib)).wait_send()
     remote(rows(dkvb, 0, 16 * PAD), rows(dkvb, 0, 16 * PAD), ssem.at[5], rsem.at[5], (x, sib)).wait_send()
+    remote(al.at[:, pl.ds(0, 3)], al.at[:, pl.ds(0, 3)], ssem.at[2], rsem.at[2], (x, sib)).wait_send()
     for c in outs:
         c.wait()
 
@@ -427,10 +431,9 @@
 def shards(activations, qkv_weight, out_weight, out_grad):
     any_spec = pl.BlockSpec(memory_space=pl.ANY)
     V = pltpu.VMEM
-    widths = [c[1] for c in COLS]
     scratch = [
-        V((2, 2 * PAD, D), BF),
-        V((2, D, 2 * PAD), BF),
+        V((2, 8, PAD, D), BF),
+        V((2, D, 8 * PAD), BF),
         V((D, 3 * INNER), BF),
         V((INNER, D), BF),
         V((8 * PAD, 128), BF),
@@ -450,26 +453,21 @@
         V((8 * PAD, 128), BF),
         V((8 * PAD, 128), BF),
         V((16 * PAD, 128), BF),
-        V((4, 2 * PAD, INNER), BF),
-        V((4, 4, 4, 16, D), BF),
-    ]
-    scratch += [V((3, 4, 4, 16, w), BF) for w in widths]
-    scratch += [V((4, 4, 16, w), BF) for w in widths]
-    scratch += [V((3, 4, 16, w), BF) for w in widths]
-    scratch += [V((4, 16, w), BF) for w in widths]
-    scratch += [V((3, 16, w), BF) for w in widths]
-    scratch += [
-        V((2, 2, 8, D), F32),
+        V((4, 4, PAD, 128), BF),
+        V((2, 8, PAD, 128), BF),
+        V((2, 16, 4, 16, 128), BF),
+        V((2, 15, 4, 16, 128), BF),
+        V((8, 2, 8, 128), F32),
+        V((8, 2, 8, 128), F32),
         V((TOK, D), BF),
         V((TOK, D), BF),
         V((8, 2 * D), F32),
         pltpu.SemaphoreType.DMA((8,)),
-        pltpu.SemaphoreType.DMA((9,)),
-        pltpu.SemaphoreType.DMA((9,)),
-        pltpu.SemaphoreType.DMA((9,)),
-        pltpu.SemaphoreType.DMA((9,)),
+        pltpu.SemaphoreType.DMA((13,)),
+        pltpu.SemaphoreType.DMA((13,)),
         pltpu.SemaphoreType.DMA((16,)),
         pltpu.SemaphoreType.DMA((3,)),
+        pltpu.SemaphoreType.DMA((4,)),
     ]
     made = pl.pallas_call(
         kernel,

time: 79.3 us -> 76.3 us (0.962)
  Pallas kernels: 78.5 us -> 75.4 us
    pallas_call x1, Pallas kernels: 76.7 us -> 73.6 us  [shards(): pl.pallas_call(kernel, out_shape=(jax.ShapeDtypeStruct((1, TOK, D), BF),...]
where the time goes in v4:
time: 76.3 us; the launch traced here: 76.2 us
  Pallas kernels  75.4 us (99%)
  between operations  0.8 us (1%)
    pallas_call x1, Pallas kernels, shards(): pl.pallas_call(kernel, out_shape=(jax.ShapeDtypeStruct((1, TOK, D), BF),...  73.6 us
    pallas_call x1, Pallas kernels, shards(): pl.pallas_call(hand_out, out_shape=tuple((jax.ShapeDtypeStruct(a.shape, a...  1.83 us

profile of v4, /device:TPU:1, one launch (start us, length us, event | category | flops | bytes accessed | tf_op | source)
XLA Modules:
  0.0 76.2 jit_solution(5121885207832296807)
XLA Ops:
  0.6 73.6 %attention_sublayer.1 = (bf16[1,136,1024]{2,1,0:T(8,128)(2,1)}, bf16[1,136,1024]{2,1,0:T(8,128)(2,1)}, f32[8,1536]{1,0:T(8,128)}, f32[8,512]{1,0:T(8,128)}) custom-call(bf16[1,136,1024]{2,1,0:T(8,128)(2,1)} %act_h.1, bf16[1024,1536]{1,0:T(8,128)(2,1)} %wqkv_h.1, bf16[512,1024]{1,0:T(8,128)(2,1)} %wout_h.1, bf16[1,136,1024]{2,1,0:T(8,128)(2,1)} %og_h.1), custom_call_target="tpu_custom_call" | custom-call | tf_op jit(solution)/shard_map/attention_sublayer/pallas_call | solution.py:472
  74.2 1.8 %hand_out.1 = (bf16[1,136,1024]{2,1,0:T(8,128)(2,1)}, bf16[1,136,1024]{2,1,0:T(8,128)(2,1)}, f32[8,1536]{1,0:T(8,128)}, f32[8,512]{1,0:T(8,128)}) custom-call(bf16[1,136,1024]{2,1,0:T(8,128)(2,1)} %get-tuple-element.12.refs_0_, bf16[1,136,1024]{2,1,0:T(8,128)(2,1)} %get-tuple-element.13.refs_1_, f32[8,1536]{1,0:T(8,128)} %get-tuple-element.14.refs_2_, ...), custom_call_target="tpu_custom_call" | custom-call | tf_op jit(solution)/shard_map/hand_out/pallas_call | solution.py:487

commit v5 on v4

--- a/solution.py
+++ b/solution.py
@@ -122,16 +122,6 @@
         sendkv[(2 * i) * PAD:(2 * i + 1) * PAD, :] = a.astype(BF)
         sendkv[(2 * i + 1) * PAD:(2 * i + 2) * PAD, :] = b.astype(BF)
 
-    pl.semaphore_wait(bar, 22)
-    own_kv = pltpu.make_async_copy(rows(sendkv, head * PAD), kvslot(s), lsem.at[4])
-    own_kv.start()
-    remote(rows(sendkv, head * PAD), kvslot(s), ssem.at[3], rsem.at[3], (x, sib)).start()
-
-    @pl.loop(1, 16)
-    def _(k):
-        to = (pos + k) % 16
-        remote(rows(sendkv, (to // 2) * PAD), kvslot(s), ssem.at[0], ksem.at[pos], (x, 2 * to + core)).start()
-
     cin[2].wait()
     cin[3].wait()
     qp = dot(al[0, spot], wqkv[:, 0:INNER])
@@ -141,21 +131,6 @@
         sendqg[(2 * i) * PAD:(2 * i + 1) * PAD, :] = a.astype(BF)
         sendqg[(2 * i + 1) * PAD:(2 * i + 2) * PAD, :] = b.astype(BF)
 
-    @pl.loop(1, 4)
-    def _(k):
-        remote(al.at[:, spot], al.at[:, spot], ssem.at[2], xsem.at[x], ((x + k) % 4, s)).start()
-
-    remote(al.at[:, spot], al.at[:, spot], ssem.at[7], rsem.at[7], (x, sib)).start()
-
-    slot = 7 - s // 4
-    own_qg = pltpu.make_async_copy(rows(sendqg, head * PAD), rows(qg, slot * PAD), lsem.at[5])
-    own_qg.start()
-
-    @pl.loop(1, 8)
-    def _(k):
-        to = (head + k) % 8
-        remote(rows(sendqg, to * PAD), rows(qg, slot * PAD), ssem.at[1], rsem.at[1], (x, 4 * to + quarter)).start()
-
     lo, hi = lane_bounds(PAD)
     place = lax.broadcasted_iota(jnp.int32, (PAD, 128), 0)
 
@@ -164,6 +139,31 @@
         t = jnp.where(place < TOK, place + g * TOK, FAR)
         kvx[pl.ds(pl.multiple_of(g * PAD, 16), PAD), 128:256] = jnp.where(
             (t >= lo) & (t < hi), 1.0, 0.0).astype(BF)
+
+    pl.semaphore_wait(bar, 22)
+    own_kv = pltpu.make_async_copy(rows(sendkv, head * PAD), kvslot(s), lsem.at[4])
+    own_kv.start()
+    remote(rows(sendkv, head * PAD), kvslot(s), ssem.at[3], rsem.at[3], (x, sib)).start()
+
+    @pl.loop(1, 16)
+    def _(k):
+        to = (pos + k) % 16
+        remote(rows(sendkv, (to // 2) * PAD), kvslot(s), ssem.at[0], ksem.at[pos], (x, 2 * to + core)).start()
+
+    @pl.loop(1, 4)
+    def _(k):
+        remote(al.at[:, spot], al.at[:, spot], ssem.at[2], xsem.at[x], ((x + k) % 4, s)).start()
+
+    remote(al.at[:, spot], al.at[:, spot], ssem.at[7], rsem.at[7], (x, sib)).start()
+
+    slot = 7 - s // 4
+    own_qg = pltpu.make_async_copy(rows(sendqg, head * PAD), rows(qg, slot * PAD), lsem.at[5])
+    own_qg.start()
+
+    @pl.loop(1, 8)
+    def _(k):
+        to = (head + k) % 8
+        remote(rows(sendqg, to * PAD), rows(qg, slot * PAD), ssem.at[1], rsem.at[1], (x, 4 * to + quarter)).start()
 
     @pl.loop(1, 16)
     def _(k):
@@ -246,6 +246,14 @@
             p = jnp.exp(sbuf[0:count, kk] - row_max).astype(BF)
             pbuf[0:count, kk] = p
             acc[0:count, :] += dot(p, kvx[kk, :])
+
+        if number == 2:
+            @pl.loop(1, 4)
+            def _(k):
+                frm = (x + k) % 4
+                q = 2 * frm + core
+                remote(al.at[:, q], al.at[:, q], ssem.at[2], xsem.at[frm], (x, sib)).wait_recv()
+                remote(al.at[:, q], al.at[:, q], ssem.at[7], rsem.at[7], (x, sib)).start()
 
         lane = lax.broadcasted_iota(jnp.int32, (count, 128), 1)
         near = lane < 64
@@ -293,13 +301,7 @@
 
         finish(lo_group, hi_group)
         to_sibling(number, lo_group, hi_group)
-        if number == 1:
-            @pl.loop(1, 4)
-            def _(k):
-                frm = (x + k) % 4
-                q = 2 * frm + core
-                remote(al.at[:, q], al.at[:, q], ssem.at[2], xsem.at[frm], (x, sib)).wait_recv()
-                remote(al.at[:, q], al.at[:, q], ssem.at[7], rsem.at[7], (x, sib)).start()
+    to_owners(len(BATCHES) - 1, *BATCHES[-1][4:])
 
     remote(al.at[:, pl.ds(0, 4)], al.at[:, pl.ds(0, 4)], ssem.at[7], rsem.at[7], (x, sib)).wait()
 
@@ -312,8 +314,6 @@
     @pl.when(core == 1)
     def _():
         transpose_inputs(1)
-
-    to_owners(len(BATCHES) - 1, *BATCHES[-1][4:])
 
     pltpu.make_async_copy(rows(resb, 0), rows(rqc, 0), lsem.at[6]).wait()
     remote(rows(rqc, 0, 7 * PAD), rows(rqc, 0, 7 * PAD), ssem.at[4], rsem.at[4], (x, sib)).wait()
@@ -372,7 +372,6 @@
         pltpu.make_async_copy(wob.at[:, pl.ds(3 * INNER, INNER)], wo_o, lsem.at[3]),
     ]
     outs[0].start()
-    partial_sums(0, early, core)
 
     pltpu.make_async_copy(rows(dkvb, 0), rows(rkv, 0), lsem.at[7]).wait()
     remote(rows(rkv, 0, 15 * PAD), rows(rkv, 0, 15 * PAD), ssem.at[6], rsem.at[6], (x, sib)).wait()
@@ -389,6 +388,7 @@
     ing += dot_nt(wide(2), wqkv[:, 2 * INNER:])
     ingb[...] = ing[0:TOK].astype(BF)
     outs[1].start()
+    partial_sums(0, early, core)
     partial_sums(1, late, 0)
     sums(0)
     sums(1)

time: 76.3 us -> 72.6 us (0.952)
  Pallas kernels: 75.4 us -> 71.6 us
    pallas_call x1, Pallas kernels: 73.6 us -> 69.8 us  [shards(): pl.pallas_call(kernel, out_shape=(jax.ShapeDtypeStruct((1, TOK, D), BF),...]
where the time goes in v5:
time: 72.6 us; the launch traced here: 72.4 us
  Pallas kernels  71.6 us (99%)
  between operations  0.8 us (1%)
    pallas_call x1, Pallas kernels, shards(): pl.pallas_call(kernel, out_shape=(jax.ShapeDtypeStruct((1, TOK, D), BF),...  69.8 us
    pallas_call x1, Pallas kernels, shards(): pl.pallas_call(hand_out, out_shape=tuple((jax.ShapeDtypeStruct(a.shape, a...  1.83 us

profile of v5, /device:TPU:1, one launch (start us, length us, event | category | flops | bytes accessed | tf_op | source)
XLA Modules:
  0.0 72.4 jit_solution(16557213264848932024)
XLA Ops:
  0.6 69.8 %attention_sublayer.1 = (bf16[1,136,1024]{2,1,0:T(8,128)(2,1)}, bf16[1,136,1024]{2,1,0:T(8,128)(2,1)}, f32[8,1536]{1,0:T(8,128)}, f32[8,512]{1,0:T(8,128)}) custom-call(bf16[1,136,1024]{2,1,0:T(8,128)(2,1)} %act_h.1, bf16[1024,1536]{1,0:T(8,128)(2,1)} %wqkv_h.1, bf16[512,1024]{1,0:T(8,128)(2,1)} %wout_h.1, bf16[1,136,1024]{2,1,0:T(8,128)(2,1)} %og_h.1), custom_call_target="tpu_custom_call" | custom-call | tf_op jit(solution)/shard_map/attention_sublayer/pallas_call | solution.py:472
  70.4 1.8 %hand_out.1 = (bf16[1,136,1024]{2,1,0:T(8,128)(2,1)}, bf16[1,136,1024]{2,1,0:T(8,128)(2,1)}, f32[8,1536]{1,0:T(8,128)}, f32[8,512]{1,0:T(8,128)}) custom-call(bf16[1,136,1024]{2,1,0:T(8,128)(2,1)} %get-tuple-element.12.refs_0_, bf16[1,136,1024]{2,1,0:T(8,128)(2,1)} %get-tuple-element.13.refs_1_, f32[8,1536]{1,0:T(8,128)} %get-tuple-element.14.refs_2_, ...), custom_call_target="tpu_custom_call" | custom-call | tf_op jit(solution)/shard_map/hand_out/pallas_call | solution.py:487

commit v6 on v5

--- a/solution.py
+++ b/solution.py
@@ -67,7 +67,7 @@
 
 def kernel(act_h, wqkv_h, wout_h, og_h, att_o, ing_o, wq_o, wo_o,
            al, alT, wqkv, wout, sendkv, sendqg, kvx, qg, qx, sbuf, pbuf, macc, acc, dq,
-           qgT, dkT, dkvb, sibr, resb, rqc, rkv, catp, cgx, fb, fr, fo, fi,
+           qgT, dkT, dkvb, sibr, resb, rqc, rkv, catp, cge, cgl, cgx, fb, fr, fo, fi,
            attb, ingb, wob, lsem, ssem, rsem, ksem, dsem, xsem):
     x = lax.axis_index("dp")
     s = lax.axis_index("seq")
@@ -98,6 +98,12 @@
     def _(k):
         pl.semaphore_signal(bar, inc=1, device_id=at_spot((spot + k) % 8), device_id_type=MESH)
 
+    @pl.loop(0, 16)
+    def _(k):
+        @pl.when((k // 4 != x) | (4 * spot + k % 4 != s))
+        def _():
+            pl.semaphore_signal(bar, inc=1, device_id=(k // 4, 4 * spot + k % 4), device_id_type=MESH)
+
     for i in range(2):
         al[i, spot, TOK:PAD, :] = jnp.zeros((PAD - TOK, D), BF)
 
@@ -140,7 +146,7 @@
         kvx[pl.ds(pl.multiple_of(g * PAD, 16), PAD), 128:256] = jnp.where(
             (t >= lo) & (t < hi), 1.0, 0.0).astype(BF)
 
-    pl.semaphore_wait(bar, 22)
+    pl.semaphore_wait(bar, jnp.where(head == spot, 37, 38))
     own_kv = pltpu.make_async_copy(rows(sendkv, head * PAD), kvslot(s), lsem.at[4])
     own_kv.start()
     remote(rows(sendkv, head * PAD), kvslot(s), ssem.at[3], rsem.at[3], (x, sib)).start()
@@ -188,6 +194,29 @@
 
     part = 2 * head + (pos % 2)
 
+    def to_summer(block, place, held, group_pos, n):
+        here = (head == spot) & (group_pos == pos)
+
+        @pl.when(jnp.logical_not(here))
+        def _():
+            remote(block, rows(held, place * PAD), ssem.at[8 + n], rsem.at[8 + n],
+                   (head // 2, 2 * group_pos + head % 2)).start()
+
+        @pl.when(here)
+        def _():
+            pltpu.make_async_copy(block, rows(held, place * PAD), lsem.at[4 + n]).start()
+
+    def all_summed(held, count, n):
+        @pl.when(head == spot)
+        def _():
+            some = rows(held, 0, (count - 1) * PAD)
+            remote(some, some, ssem.at[8 + n], rsem.at[8 + n], (x, sib)).wait()
+            pltpu.make_async_copy(rows(dkvb, 0), rows(held, 0), lsem.at[4 + n]).wait()
+
+        @pl.when(head != spot)
+        def _():
+            remote(held, held, ssem.at[8 + n], rsem.at[8 + n], (x, sib)).wait()
+
     def finish(lo_group, hi_group):
         lo_row, hi_row = lo_group * PAD, hi_group * PAD
         for blk in range(lo_row // 128, -(-hi_row // 128)):
@@ -218,6 +247,8 @@
             @pl.when(k == pos)
             def _():
                 pltpu.make_async_copy(rows(dkvb, g * PAD), rows(rkv, part * PAD), lsem.at[7]).start()
+
+            to_summer(rows(dkvb, g * PAD), 2 * spot + pos % 2, cgl, k, 1)
 
     for number, (slot0, slots, keys, CHUNK, lo_group, hi_group) in enumerate(BATCHES):
         row0, count = slot0 * PAD, slots * PAD
@@ -299,6 +330,8 @@
             def _():
                 pltpu.make_async_copy(rows(resb, j * PAD), rows(rqc, head * PAD), lsem.at[6]).start()
 
+            to_summer(rows(resb, j * PAD), spot, cge, 2 * to + quarter // 2, 0)
+
         finish(lo_group, hi_group)
         to_sibling(number, lo_group, hi_group)
     to_owners(len(BATCHES) - 1, *BATCHES[-1][4:])
@@ -310,10 +343,23 @@
             alT[i, 128 * j:128 * j + 128, :] = al[i, :, :, 128 * j:128 * j + 128].reshape(8 * PAD, 128).T
 
     transpose_inputs(0)
-
-    @pl.when(core == 1)
-    def _():
-        transpose_inputs(1)
+    transpose_inputs(1)
+
+    def reduced(u, i, f):
+        fb[u, :, i] = f.astype(BF).reshape(16, 16, 128)
+
+    def spread(u):
+        @pl.loop(1, 16)
+        def _(k):
+            to = (pos + k) % 16
+            remote(fb.at[u, to], fr.at[u, k - 1], ssem.at[10 + u], rsem.at[10 + u], (x, 2 * to + core)).start()
+
+    all_summed(cge, 8, 0)
+    wide_left = lax.broadcasted_iota(jnp.int32, (256, 128), 1) < 64
+    for i in range(4):
+        rr = slice(256 * i, 256 * i + 256)
+        reduced(0, i, jnp.where(wide_left, dot(alT[0, rr, :], cge[...]), dot(alT[1, rr, :], cge[...])))
+    spread(0)
 
     pltpu.make_async_copy(rows(resb, 0), rows(rqc, 0), lsem.at[6]).wait()
     remote(rows(rqc, 0, 7 * PAD), rows(rqc, 0, 7 * PAD), ssem.at[4], rsem.at[4], (x, sib)).wait()
@@ -327,42 +373,6 @@
     def wide(i):
         return jnp.concatenate([catp[i, j] for j in range(4)], axis=1)
 
-    def exchange(u, blocks):
-        own = pltpu.make_async_copy(catp.at[blocks[0] + (blocks[1] - blocks[0]) * core, x], cgx.at[u, spot], lsem.at[4 + u])
-        own.start()
-
-        @pl.loop(1, 8)
-        def _(k):
-            q = (spot + k) % 8
-            block = blocks[0] + (blocks[1] - blocks[0]) * (q % 2)
-            remote(catp.at[block, q // 2], cgx.at[u, spot], ssem.at[8 + u], rsem.at[8 + u], at_spot(q)).start()
-
-        return own
-
-    def partial_sums(u, own, lhs):
-        own.wait()
-        seven = cgx.at[u, pl.ds(0, 7)]
-        remote(seven, seven, ssem.at[8 + u], rsem.at[8 + u], (x, sib)).wait()
-        right = cgx[u].reshape(8 * PAD, 128)
-        for i in range(4):
-            f = dot(alT[lhs, 256 * i:256 * i + 256, :], right)
-            fb[u, :, i] = f.astype(BF).reshape(16, 16, 128)
-
-        @pl.loop(1, 16)
-        def _(k):
-            to = (pos + k) % 16
-            remote(fb.at[u, to], fr.at[u, k - 1], ssem.at[10 + u], rsem.at[10 + u], (x, 2 * to + core)).start()
-
-    def sums(u):
-        remote(fr.at[u], fr.at[u], ssem.at[10 + u], rsem.at[10 + u], (x, sib)).wait()
-        v = fb[u, pos].astype(F32)
-        for k in range(15):
-            v += fr[u, k].astype(F32)
-        for i in range(4):
-            for c in range(2):
-                fo[2 * i + c, u] = v[i, 8 * c:8 * c + 8]
-
-    early = exchange(0, (0, 3))
     att = dot(wide(3), wout[...])
     attb[...] = att[0:TOK].astype(BF)
     outs = [
@@ -373,6 +383,15 @@
     ]
     outs[0].start()
 
+    all_summed(cgl, 16, 1)
+    for q in range(8):
+        cgx[q * PAD:(q + 1) * PAD, :] = (
+            cgl[(2 * q) * PAD:(2 * q + 1) * PAD, :].astype(F32) + cgl[(2 * q + 1) * PAD:(2 * q + 2) * PAD, :].astype(F32)
+        ).astype(BF)
+    for i in range(4):
+        reduced(1, i, dot(alT[0, 256 * i:256 * i + 256, :], cgx[...]))
+    spread(1)
+
     pltpu.make_async_copy(rows(dkvb, 0), rows(rkv, 0), lsem.at[7]).wait()
     remote(rows(rkv, 0, 15 * PAD), rows(rkv, 0, 15 * PAD), ssem.at[6], rsem.at[6], (x, sib)).wait()
     for i in range(4):
@@ -382,14 +401,20 @@
         catp[1, i] = k_pair.astype(BF)
         catp[2, i] = v_pair.astype(BF)
 
-    late = exchange(1, (1, 2))
     ing = dot_nt(wide(0), wqkv[:, 0:INNER])
     ing += dot_nt(wide(1), wqkv[:, INNER:2 * INNER])
     ing += dot_nt(wide(2), wqkv[:, 2 * INNER:])
     ingb[...] = ing[0:TOK].astype(BF)
     outs[1].start()
-    partial_sums(0, early, core)
-    partial_sums(1, late, 0)
+    def sums(u):
+        remote(fr.at[u], fr.at[u], ssem.at[10 + u], rsem.at[10 + u], (x, sib)).wait()
+        v = fb[u, pos].astype(F32)
+        for k in range(15):
+            v += fr[u, k].astype(F32)
+        for i in range(4):
+            for c in range(2):
+                fo[2 * i + c, u] = v[i, 8 * c:8 * c + 8]
+
     sums(0)
     sums(1)
 
@@ -402,8 +427,10 @@
 
     remote(fi.at[pl.ds(0, 7)], fi.at[pl.ds(0, 7)], ssem.at[12], rsem.at[12], (x, sib)).wait()
     for i in range(4):
-        for block, (c, u) in enumerate(((0, 0), (0, 1), (1, 1), (1, 0))):
-            wob[:, INNER * block + 128 * i:INNER * block + 128 * i + 128] = fi[2 * i + c, u]
+        for u, blocks in enumerate(((0, 3), (1, 2))):
+            pair = swap_pack(fi[2 * i, u], fi[2 * i + 1, u], left[0:8])
+            for block, v in zip(blocks, pair):
+                wob[:, INNER * block + 128 * i:INNER * block + 128 * i + 128] = v
     outs[2].start()
     outs[3].start()
 
@@ -454,7 +481,9 @@
         V((8 * PAD, 128), BF),
         V((16 * PAD, 128), BF),
         V((4, 4, PAD, 128), BF),
-        V((2, 8, PAD, 128), BF),
+        V((8 * PAD, 128), BF),
+        V((16 * PAD, 128), BF),
+        V((8 * PAD, 128), BF),
         V((2, 16, 4, 16, 128), BF),
         V((2, 15, 4, 16, 128), BF),
         V((8, 2, 8, 128), F32),

time: 72.6 us -> 101 us (1.39)
  Pallas kernels: 71.6 us -> 99.8 us
    pallas_call x1, Pallas kernels: 69.8 us -> 98 us  [shards(): pl.pallas_call(kernel, out_shape=(jax.ShapeDtypeStruct((1, TOK, D), BF),...]
where the time goes in v6:
time: 101 us
  Pallas kernels  99.8 us (99%)
    pallas_call x1, Pallas kernels, shards(): pl.pallas_call(kernel, out_shape=(jax.ShapeDtypeStruct((1, TOK, D), BF),...  98 us

profile of v6, /device:TPU:1, one launch (start us, length us, event | category | flops | bytes accessed | tf_op | source)
XLA Modules:
  0.0 100.6 jit_solution(2545357451592975577)
XLA Ops:
  0.6 98.0 %attention_sublayer.1 = (bf16[1,136,1024]{2,1,0:T(8,128)(2,1)}, bf16[1,136,1024]{2,1,0:T(8,128)(2,1)}, f32[8,1536]{1,0:T(8,128)}, f32[8,512]{1,0:T(8,128)}) custom-call(bf16[1,136,1024]{2,1,0:T(8,128)(2,1)} %act_h.1, bf16[1024,1536]{1,0:T(8,128)(2,1)} %wqkv_h.1, bf16[512,1024]{1,0:T(8,128)(2,1)} %wout_h.1, bf16[1,136,1024]{2,1,0:T(8,128)(2,1)} %og_h.1), custom_call_target="tpu_custom_call" | custom-call | tf_op jit(solution)/shard_map/attention_sublayer/pallas_call | solution.py:501
  98.6 1.8 %hand_out.1 = (bf16[1,136,1024]{2,1,0:T(8,128)(2,1)}, bf16[1,136,1024]{2,1,0:T(8,128)(2,1)}, f32[8,1536]{1,0:T(8,128)}, f32[8,512]{1,0:T(8,128)}) custom-call(bf16[1,136,1024]{2,1,0:T(8,128)(2,1)} %get-tuple-element.12.refs_0_, bf16[1,136,1024]{2,1,0:T(8,128)(2,1)} %get-tuple-element.13.refs_1_, f32[8,1536]{1,0:T(8,128)} %get-tuple-element.14.refs_2_, ...), custom_call_target="tpu_custom_call" | custom-call | tf_op jit(solution)/shard_map/hand_out/pallas_call | solution.py:516

commit v7 on v6

--- a/solution.py
+++ b/solution.py
@@ -98,11 +98,20 @@
     def _(k):
         pl.semaphore_signal(bar, inc=1, device_id=at_spot((spot + k) % 8), device_id_type=MESH)
 
+    def summer(h, at):
+        return (h // 2 + at // 4 + at % 4) % 4, 2 * at + h % 2
+
+    mine = 2 * ((x + 8 - pos // 4 - pos % 4) % 4) + core
+
     @pl.loop(0, 16)
     def _(k):
-        @pl.when((k // 4 != x) | (4 * spot + k % 4 != s))
+        @pl.when((k // 4 != x) | (4 * mine + k % 4 != s))
         def _():
-            pl.semaphore_signal(bar, inc=1, device_id=(k // 4, 4 * spot + k % 4), device_id_type=MESH)
+            pl.semaphore_signal(bar, inc=1, device_id=(k // 4, 4 * mine + k % 4), device_id_type=MESH)
+
+    @pl.loop(1, 16)
+    def _(k):
+        pl.semaphore_signal(bar, inc=1, device_id=summer(mine, (pos + k) % 16), device_id_type=MESH)
 
     for i in range(2):
         al[i, spot, TOK:PAD, :] = jnp.zeros((PAD - TOK, D), BF)
@@ -146,7 +155,7 @@
         kvx[pl.ds(pl.multiple_of(g * PAD, 16), PAD), 128:256] = jnp.where(
             (t >= lo) & (t < hi), 1.0, 0.0).astype(BF)
 
-    pl.semaphore_wait(bar, jnp.where(head == spot, 37, 38))
+    pl.semaphore_wait(bar, jnp.where(head == mine, 52, 53))
     own_kv = pltpu.make_async_copy(rows(sendkv, head * PAD), kvslot(s), lsem.at[4])
     own_kv.start()
     remote(rows(sendkv, head * PAD), kvslot(s), ssem.at[3], rsem.at[3], (x, sib)).start()
@@ -195,25 +204,25 @@
     part = 2 * head + (pos % 2)
 
     def to_summer(block, place, held, group_pos, n):
-        here = (head == spot) & (group_pos == pos)
+        here = (head == mine) & (group_pos == pos)
 
         @pl.when(jnp.logical_not(here))
         def _():
             remote(block, rows(held, place * PAD), ssem.at[8 + n], rsem.at[8 + n],
-                   (head // 2, 2 * group_pos + head % 2)).start()
+                   summer(head, group_pos)).start()
 
         @pl.when(here)
         def _():
             pltpu.make_async_copy(block, rows(held, place * PAD), lsem.at[4 + n]).start()
 
     def all_summed(held, count, n):
-        @pl.when(head == spot)
+        @pl.when(head == mine)
         def _():
             some = rows(held, 0, (count - 1) * PAD)
             remote(some, some, ssem.at[8 + n], rsem.at[8 + n], (x, sib)).wait()
             pltpu.make_async_copy(rows(dkvb, 0), rows(held, 0), lsem.at[4 + n]).wait()
 
-        @pl.when(head != spot)
+        @pl.when(head != mine)
         def _():
             remote(held, held, ssem.at[8 + n], rsem.at[8 + n], (x, sib)).wait()
 
@@ -352,7 +361,7 @@
         @pl.loop(1, 16)
         def _(k):
             to = (pos + k) % 16
-            remote(fb.at[u, to], fr.at[u, k - 1], ssem.at[10 + u], rsem.at[10 + u], (x, 2 * to + core)).start()
+            remote(fb.at[u, to], fr.at[u, k - 1], ssem.at[10 + u], rsem.at[10 + u], summer(mine, to)).start()
 
     all_summed(cge, 8, 0)
     wide_left = lax.broadcasted_iota(jnp.int32, (256, 128), 1) < 64
@@ -418,12 +427,12 @@
     sums(0)
     sums(1)
 
-    fi[spot] = fo[spot]
+    fi[mine] = fo[spot]
 
     @pl.loop(1, 8)
     def _(k):
         q = (spot + k) % 8
-        remote(fo.at[q], fi.at[spot], ssem.at[12], rsem.at[12], at_spot(q)).start()
+        remote(fo.at[q], fi.at[mine], ssem.at[12], rsem.at[12], at_spot(q)).start()
 
     remote(fi.at[pl.ds(0, 7)], fi.at[pl.ds(0, 7)], ssem.at[12], rsem.at[12], (x, sib)).wait()
     for i in range(4):

time: 101 us -> 82 us (0.81)
  Pallas kernels: 99.8 us -> 81.1 us
    pallas_call x1, Pallas kernels: 98 us -> 79.3 us  [shards(): pl.pallas_call(kernel, out_shape=(jax.ShapeDtypeStruct((1, TOK, D), BF),...]
where the time goes in v7:
time: 82 us; the launch traced here: 81.9 us
  Pallas kernels  81.1 us (99%)
    pallas_call x1, Pallas kernels, shards(): pl.pallas_call(kernel, out_shape=(jax.ShapeDtypeStruct((1, TOK, D), BF),...  79.3 us
    pallas_call x1, Pallas kernels, shards(): pl.pallas_call(hand_out, out_shape=tuple((jax.ShapeDtypeStruct(a.shape, a...  1.83 us

profile of v7, /device:TPU:1, one launch (start us, length us, event | category | flops | bytes accessed | tf_op | source)
XLA Modules:
  0.0 81.9 jit_solution(13211821595970151041)
XLA Ops:
  0.6 79.3 %attention_sublayer.1 = (bf16[1,136,1024]{2,1,0:T(8,128)(2,1)}, bf16[1,136,1024]{2,1,0:T(8,128)(2,1)}, f32[8,1536]{1,0:T(8,128)}, f32[8,512]{1,0:T(8,128)}) custom-call(bf16[1,136,1024]{2,1,0:T(8,128)(2,1)} %act_h.1, bf16[1024,1536]{1,0:T(8,128)(2,1)} %wqkv_h.1, bf16[512,1024]{1,0:T(8,128)(2,1)} %wout_h.1, bf16[1,136,1024]{2,1,0:T(8,128)(2,1)} %og_h.1), custom_call_target="tpu_custom_call" | custom-call | tf_op jit(solution)/shard_map/attention_sublayer/pallas_call | solution.py:510
  79.9 1.8 %hand_out.1 = (bf16[1,136,1024]{2,1,0:T(8,128)(2,1)}, bf16[1,136,1024]{2,1,0:T(8,128)(2,1)}, f32[8,1536]{1,0:T(8,128)}, f32[8,512]{1,0:T(8,128)}) custom-call(bf16[1,136,1024]{2,1,0:T(8,128)(2,1)} %get-tuple-element.12.refs_0_, bf16[1,136,1024]{2,1,0:T(8,128)(2,1)} %get-tuple-element.13.refs_1_, f32[8,1536]{1,0:T(8,128)} %get-tuple-element.14.refs_2_, ...), custom_call_target="tpu_custom_call" | custom-call | tf_op jit(solution)/shard_map/hand_out/pallas_call | solution.py:525

commit v8 on v5

--- a/solution.py
+++ b/solution.py
@@ -25,6 +25,7 @@
 STARTS = [0] + ENDS[:-1]
 FAR = 1 << 20
 BIG = 1e30
+TILES = ((224, 208), (144, 144), (224, 208))
 ONE = 15
 TWO = 16
 BATCHES = (
@@ -66,7 +67,7 @@
 
 
 def kernel(act_h, wqkv_h, wout_h, og_h, att_o, ing_o, wq_o, wo_o,
-           al, alT, wqkv, wout, sendkv, sendqg, kvx, qg, qx, sbuf, pbuf, macc, acc, dq,
+           al, alT, wqkv, wout, sendkv, sendqg, kvx, qg, qx, pbuf, acc, dq,
            qgT, dkT, dkvb, sibr, resb, rqc, rkv, catp, cgx, fb, fr, fo, fi,
            attb, ingb, wob, lsem, ssem, rsem, ksem, dsem, xsem):
     x = lax.axis_index("dp")
@@ -222,31 +223,17 @@
     for number, (slot0, slots, keys, CHUNK, lo_group, hi_group) in enumerate(BATCHES):
         row0, count = slot0 * PAD, slots * PAD
         rr = slice(row0, row0 + count)
-        steps = keys // CHUNK
-        macc[0:count, :] = jnp.full((count, 128), -3e38, F32)
-
-        @pl.loop(0, steps)
-        def _(c):
-            kk = pl.ds(pl.multiple_of(c * CHUNK, 128), CHUNK)
-            sc = dot_nt(qx[rr, :], kvx[kk, :])
-            sbuf[0:count, kk] = sc
-            top = macc[0:count, :]
-            for i in range(CHUNK // 128):
-                top = jnp.maximum(top, sc[:, 128 * i:128 * i + 128])
-            macc[0:count, :] = top
-
-        if number > 0:
-            to_owners(number - 1, *BATCHES[number - 1][4:])
-        row_max = jnp.max(macc[0:count, :], axis=1, keepdims=True)
-        acc[0:count, :] = jnp.zeros((count, 256), F32)
-
-        @pl.loop(0, steps)
-        def _(c):
-            kk = pl.ds(pl.multiple_of(c * CHUNK, 128), CHUNK)
-            p = jnp.exp(sbuf[0:count, kk] - row_max).astype(BF)
-            pbuf[0:count, kk] = p
-            acc[0:count, :] += dot(p, kvx[kk, :])
-
+        ends = np.cumsum((0,) + TILES[number])
+        scores = [dot_nt(qx[row0:row0 + ends[1], :], kvx[0:keys, :])]
+        for i, (a, b) in enumerate(zip(ends[:-1], ends[1:])):
+            if i + 2 < len(ends):
+                scores.append(dot_nt(qx[row0 + b:row0 + ends[i + 2], :], kvx[0:keys, :]))
+            row_max = jnp.max(scores[i], axis=1, keepdims=True)
+            p = jnp.exp(scores[i] - row_max).astype(BF)
+            pbuf[a:b, 0:keys] = p
+            acc[a:b, :] = dot(p, kvx[0:keys, :])
+            if i == 0 and number > 0:
+                to_owners(number - 1, *BATCHES[number - 1][4:])
         if number == 2:
             @pl.loop(1, 4)
             def _(k):
@@ -269,14 +256,17 @@
         qgT[:, 0:count] = qn.T.astype(BF)
         dq[0:count, :] = jnp.zeros((count, 128), F32)
 
-        @pl.loop(0, steps)
-        def _(c):
-            kk = pl.ds(pl.multiple_of(c * CHUNK, 128), CHUNK)
+        parts = [slice(c * CHUNK, (c + 1) * CHUNK) for c in range(keys // CHUNK)]
+        dpd = [dot_nt(qx[rr, :], kvx[parts[0], :])]
+        ds = []
+        for c, kk in enumerate(parts):
+            if c + 1 < len(parts):
+                dpd.append(dot_nt(qx[rr, :], kvx[parts[c + 1], :]))
             p = pbuf[0:count, kk]
-            dpd = dot_nt(qx[rr, :], kvx[kk, :])
-            ds = (p.astype(F32) * dpd).astype(BF)
-            dq[0:count, :] += dot(ds, kvx[kk, 0:128])
-            dk = dot(qgT[0:64, 0:count], ds)
+            ds.append((p.astype(F32) * dpd[c]).astype(BF))
+            if number < 2:
+                dq[0:count, :] += dot(ds[c], kvx[kk, 0:128])
+            dk = dot(qgT[0:64, 0:count], ds[c])
             dv = dot(qgT[64:128, 0:count], p)
             if number == 0:
                 dkT[0:64, kk] = dk
@@ -285,6 +275,11 @@
                 dkT[0:64, kk] += dk
                 dkT[64:128, kk] += dv
 
+        if number == 2:
+            finish(lo_group, hi_group)
+            to_sibling(number, lo_group, hi_group)
+            for c, kk in enumerate(parts):
+                dq[0:count, :] += dot(ds[c], kvx[kk, 0:128])
         resb[rr, :] = jnp.where(near, dq[0:count, :] * (0.125 * inv), ctx.astype(F32)).astype(BF)
 
         for j in range(slot0, slot0 + slots):
@@ -299,8 +294,9 @@
             def _():
                 pltpu.make_async_copy(rows(resb, j * PAD), rows(rqc, head * PAD), lsem.at[6]).start()
 
-        finish(lo_group, hi_group)
-        to_sibling(number, lo_group, hi_group)
+        if number < 2:
+            finish(lo_group, hi_group)
+            to_sibling(number, lo_group, hi_group)
     to_owners(len(BATCHES) - 1, *BATCHES[-1][4:])
 
     remote(al.at[:, pl.ds(0, 4)], al.at[:, pl.ds(0, 4)], ssem.at[7], rsem.at[7], (x, sib)).wait()
@@ -441,9 +437,7 @@
         V((KEYS, 256), BF),
         V((8 * PAD, 128), BF),
         V((8 * PAD, 256), BF),
-        V((3 * PAD, KEYS), F32),
         V((3 * PAD, KEYS), BF),
-        V((3 * PAD, 128), F32),
         V((3 * PAD, 256), F32),
         V((3 * PAD, 128), F32),
         V((128, 3 * PAD), BF),

time: 72.6 us -> 73.8 us (1.017)
  Pallas kernels: 71.6 us -> 72.8 us
    pallas_call x1, Pallas kernels: 69.8 us -> 71 us  [shards(): pl.pallas_call(kernel, out_shape=(jax.ShapeDtypeStruct((1, TOK, D), BF),...]
where the time goes in v8:
time: 73.8 us; the launch traced here: 73.6 us
  Pallas kernels  72.8 us (99%)
  between operations  0.8 us (1%)
    pallas_call x1, Pallas kernels, shards(): pl.pallas_call(kernel, out_shape=(jax.ShapeDtypeStruct((1, TOK, D), BF),...  71 us
    pallas_call x1, Pallas kernels, shards(): pl.pallas_call(hand_out, out_shape=tuple((jax.ShapeDtypeStruct(a.shape, a...  1.83 us

profile of v8, /device:TPU:1, one launch (start us, length us, event | category | flops | bytes accessed | tf_op | source)
XLA Modules:
  0.0 73.6 jit_solution(1807005038146264812)
XLA Ops:
  0.6 71.0 %attention_sublayer.1 = (bf16[1,136,1024]{2,1,0:T(8,128)(2,1)}, bf16[1,136,1024]{2,1,0:T(8,128)(2,1)}, f32[8,1536]{1,0:T(8,128)}, f32[8,512]{1,0:T(8,128)}) custom-call(bf16[1,136,1024]{2,1,0:T(8,128)(2,1)} %act_h.1, bf16[1024,1536]{1,0:T(8,128)(2,1)} %wqkv_h.1, bf16[512,1024]{1,0:T(8,128)(2,1)} %wout_h.1, bf16[1,136,1024]{2,1,0:T(8,128)(2,1)} %og_h.1), custom_call_target="tpu_custom_call" | custom-call | tf_op jit(solution)/shard_map/attention_sublayer/pallas_call | solution.py:466
  71.6 1.8 %hand_out.1 = (bf16[1,136,1024]{2,1,0:T(8,128)(2,1)}, bf16[1,136,1024]{2,1,0:T(8,128)(2,1)}, f32[8,1536]{1,0:T(8,128)}, f32[8,512]{1,0:T(8,128)}) custom-call(bf16[1,136,1024]{2,1,0:T(8,128)(2,1)} %get-tuple-element.12.refs_0_, bf16[1,136,1024]{2,1,0:T(8,128)(2,1)} %get-tuple-element.13.refs_1_, f32[8,1536]{1,0:T(8,128)} %get-tuple-element.14.refs_2_, ...), custom_call_target="tpu_custom_call" | custom-call | tf_op jit(solution)/shard_map/hand_out/pallas_call | solution.py:481

commit v9 on v8

--- a/solution.py
+++ b/solution.py
@@ -232,16 +232,8 @@
             p = jnp.exp(scores[i] - row_max).astype(BF)
             pbuf[a:b, 0:keys] = p
             acc[a:b, :] = dot(p, kvx[0:keys, :])
-            if i == 0 and number > 0:
-                to_owners(number - 1, *BATCHES[number - 1][4:])
-        if number == 2:
-            @pl.loop(1, 4)
-            def _(k):
-                frm = (x + k) % 4
-                q = 2 * frm + core
-                remote(al.at[:, q], al.at[:, q], ssem.at[2], xsem.at[frm], (x, sib)).wait_recv()
-                remote(al.at[:, q], al.at[:, q], ssem.at[7], rsem.at[7], (x, sib)).start()
-
+        if number > 0:
+            to_owners(number - 1, *BATCHES[number - 1][4:])
         lane = lax.broadcasted_iota(jnp.int32, (count, 128), 1)
         near = lane < 64
         inv = 1.0 / acc[0:count, 128 + ONE:128 + ONE + 1]
@@ -264,8 +256,7 @@
                 dpd.append(dot_nt(qx[rr, :], kvx[parts[c + 1], :]))
             p = pbuf[0:count, kk]
             ds.append((p.astype(F32) * dpd[c]).astype(BF))
-            if number < 2:
-                dq[0:count, :] += dot(ds[c], kvx[kk, 0:128])
+            dq[0:count, :] += dot(ds[c], kvx[kk, 0:128])
             dk = dot(qgT[0:64, 0:count], ds[c])
             dv = dot(qgT[64:128, 0:count], p)
             if number == 0:
@@ -275,11 +266,6 @@
                 dkT[0:64, kk] += dk
                 dkT[64:128, kk] += dv
 
-        if number == 2:
-            finish(lo_group, hi_group)
-            to_sibling(number, lo_group, hi_group)
-            for c, kk in enumerate(parts):
-                dq[0:count, :] += dot(ds[c], kvx[kk, 0:128])
         resb[rr, :] = jnp.where(near, dq[0:count, :] * (0.125 * inv), ctx.astype(F32)).astype(BF)
 
         for j in range(slot0, slot0 + slots):
@@ -294,10 +280,17 @@
             def _():
                 pltpu.make_async_copy(rows(resb, j * PAD), rows(rqc, head * PAD), lsem.at[6]).start()
 
-        if number < 2:
-            finish(lo_group, hi_group)
-            to_sibling(number, lo_group, hi_group)
+        finish(lo_group, hi_group)
+        to_sibling(number, lo_group, hi_group)
+
     to_owners(len(BATCHES) - 1, *BATCHES[-1][4:])
+
+    @pl.loop(1, 4)
+    def _(k):
+        frm = (x + k) % 4
+        q = 2 * frm + core
+        remote(al.at[:, q], al.at[:, q], ssem.at[2], xsem.at[frm], (x, sib)).wait_recv()
+        remote(al.at[:, q], al.at[:, q], ssem.at[7], rsem.at[7], (x, sib)).start()
 
     remote(al.at[:, pl.ds(0, 4)], al.at[:, pl.ds(0, 4)], ssem.at[7], rsem.at[7], (x, sib)).wait()
 

time: 73.8 us -> 71.7 us (0.972)
  Pallas kernels: 72.8 us -> 70.7 us
    pallas_call x1, Pallas kernels: 71 us -> 68.9 us  [shards(): pl.pallas_call(kernel, out_shape=(jax.ShapeDtypeStruct((1, TOK, D), BF),...]
where the time goes in v9:
time: 71.7 us; the launch traced here: 71.5 us
  Pallas kernels  70.7 us (99%)
  between operations  0.8 us (1%)
    pallas_call x1, Pallas kernels, shards(): pl.pallas_call(kernel, out_shape=(jax.ShapeDtypeStruct((1, TOK, D), BF),...  68.9 us
    pallas_call x1, Pallas kernels, shards(): pl.pallas_call(hand_out, out_shape=tuple((jax.ShapeDtypeStruct(a.shape, a...  1.83 us

profile of v9, /device:TPU:1, one launch (start us, length us, event | category | flops | bytes accessed | tf_op | source)
XLA Modules:
  0.0 71.5 jit_solution(2376300636552945539)
XLA Ops:
  0.6 68.9 %attention_sublayer.1 = (bf16[1,136,1024]{2,1,0:T(8,128)(2,1)}, bf16[1,136,1024]{2,1,0:T(8,128)(2,1)}, f32[8,1536]{1,0:T(8,128)}, f32[8,512]{1,0:T(8,128)}) custom-call(bf16[1,136,1024]{2,1,0:T(8,128)(2,1)} %act_h.1, bf16[1024,1536]{1,0:T(8,128)(2,1)} %wqkv_h.1, bf16[512,1024]{1,0:T(8,128)(2,1)} %wout_h.1, bf16[1,136,1024]{2,1,0:T(8,128)(2,1)} %og_h.1), custom_call_target="tpu_custom_call" | custom-call | tf_op jit(solution)/shard_map/attention_sublayer/pallas_call | solution.py:459
  69.6 1.8 %hand_out.1 = (bf16[1,136,1024]{2,1,0:T(8,128)(2,1)}, bf16[1,136,1024]{2,1,0:T(8,128)(2,1)}, f32[8,1536]{1,0:T(8,128)}, f32[8,512]{1,0:T(8,128)}) custom-call(bf16[1,136,1024]{2,1,0:T(8,128)(2,1)} %get-tuple-element.12.refs_0_, bf16[1,136,1024]{2,1,0:T(8,128)(2,1)} %get-tuple-element.13.refs_1_, f32[8,1536]{1,0:T(8,128)} %get-tuple-element.14.refs_2_, ...), custom_call_target="tpu_custom_call" | custom-call | tf_op jit(solution)/shard_map/hand_out/pallas_call | solution.py:474

commit v10 on v9

--- a/solution.py
+++ b/solution.py
@@ -292,18 +292,6 @@
         remote(al.at[:, q], al.at[:, q], ssem.at[2], xsem.at[frm], (x, sib)).wait_recv()
         remote(al.at[:, q], al.at[:, q], ssem.at[7], rsem.at[7], (x, sib)).start()
 
-    remote(al.at[:, pl.ds(0, 4)], al.at[:, pl.ds(0, 4)], ssem.at[7], rsem.at[7], (x, sib)).wait()
-
-    def transpose_inputs(i):
-        for j in range(8):
-            alT[i, 128 * j:128 * j + 128, :] = al[i, :, :, 128 * j:128 * j + 128].reshape(8 * PAD, 128).T
-
-    transpose_inputs(0)
-
-    @pl.when(core == 1)
-    def _():
-        transpose_inputs(1)
-
     pltpu.make_async_copy(rows(resb, 0), rows(rqc, 0), lsem.at[6]).wait()
     remote(rows(rqc, 0, 7 * PAD), rows(rqc, 0, 7 * PAD), ssem.at[4], rsem.at[4], (x, sib)).wait()
     for i in range(4):
@@ -352,6 +340,18 @@
                 fo[2 * i + c, u] = v[i, 8 * c:8 * c + 8]
 
     early = exchange(0, (0, 3))
+    remote(al.at[:, pl.ds(0, 4)], al.at[:, pl.ds(0, 4)], ssem.at[7], rsem.at[7], (x, sib)).wait()
+
+    def transpose_inputs(i):
+        for j in range(8):
+            alT[i, 128 * j:128 * j + 128, :] = al[i, :, :, 128 * j:128 * j + 128].reshape(8 * PAD, 128).T
+
+    transpose_inputs(0)
+
+    @pl.when(core == 1)
+    def _():
+        transpose_inputs(1)
+
     att = dot(wide(3), wout[...])
     attb[...] = att[0:TOK].astype(BF)
     outs = [

time: 71.7 us -> 71.7 us (level)
  no operation moved by 1% of the time
where the time goes in v10:
time: 71.7 us; the launch traced here: 71.5 us
  Pallas kernels  70.7 us (99%)
  between operations  0.8 us (1%)
    pallas_call x1, Pallas kernels, shards(): pl.pallas_call(kernel, out_shape=(jax.ShapeDtypeStruct((1, TOK, D), BF),...  68.9 us
    pallas_call x1, Pallas kernels, shards(): pl.pallas_call(hand_out, out_shape=tuple((jax.ShapeDtypeStruct(a.shape, a...  1.83 us

profile of v10, /device:TPU:1, one launch (start us, length us, event | category | flops | bytes accessed | tf_op | source)
XLA Modules:
  0.0 71.5 jit_solution(17806615929794747821)
XLA Ops:
  0.6 68.9 %attention_sublayer.1 = (bf16[1,136,1024]{2,1,0:T(8,128)(2,1)}, bf16[1,136,1024]{2,1,0:T(8,128)(2,1)}, f32[8,1536]{1,0:T(8,128)}, f32[8,512]{1,0:T(8,128)}) custom-call(bf16[1,136,1024]{2,1,0:T(8,128)(2,1)} %act_h.1, bf16[1024,1536]{1,0:T(8,128)(2,1)} %wqkv_h.1, bf16[512,1024]{1,0:T(8,128)(2,1)} %wout_h.1, bf16[1,136,1024]{2,1,0:T(8,128)(2,1)} %og_h.1), custom_call_target="tpu_custom_call" | custom-call | tf_op jit(solution)/shard_map/attention_sublayer/pallas_call | solution.py:459
  69.6 1.8 %hand_out.1 = (bf16[1,136,1024]{2,1,0:T(8,128)(2,1)}, bf16[1,136,1024]{2,1,0:T(8,128)(2,1)}, f32[8,1536]{1,0:T(8,128)}, f32[8,512]{1,0:T(8,128)}) custom-call(bf16[1,136,1024]{2,1,0:T(8,128)(2,1)} %get-tuple-element.12.refs_0_, bf16[1,136,1024]{2,1,0:T(8,128)(2,1)} %get-tuple-element.13.refs_1_, f32[8,1536]{1,0:T(8,128)} %get-tuple-element.14.refs_2_, ...), custom_call_target="tpu_custom_call" | custom-call | tf_op jit(solution)/shard_map/hand_out/pallas_call | solution.py:474
